TPU v7x, 32 devices: a whole 2x2x4 slice. The times are simulated.
32 devices in a mesh: groups: 1, rows: 32 (over z, y, x, core).
Axes of the slice: x: 2, y: 2, z: 4, core: 2. Of those that a mesh axis runs over, the one named last changes fastest.
Arguments:
- prompt: bfloat16 [16, 8192], P('groups'), may hold values from -6 to 6
- gate_weight: bfloat16 [8192, 4096], P(None, 'rows'), may hold values from -0.0625 to 0.0625
- up_weight: bfloat16 [8192, 4096], P(None, 'rows'), may hold values from -0.0625 to 0.0625
- down_weight: bfloat16 [4096, 8192], P('rows'), may hold values from -0.09375 to 0.09375
- proj_blocks: bfloat16 [3072, 128, 128], P('rows'), may hold values from -0.29882812 to 0.29882812
- proj_column: int32 [3072, 1], P('rows'), may hold values from 0 to 31; in each aligned block of 96 rows (0 to 95, 96 to 191, ...) at most 3 rows name the same one
- proj_row: int32 [3072], P('rows'), may hold values from 0 to 63
- proj_variant: int32 [3072], P('rows'), may hold values from 0 to 22
- proj_kind: int32 [3072], P('rows'), may hold values from 0 to 1
- down_blocks: bfloat16 [3072, 128, 128], P('rows'), may hold values from -0.59765625 to 0.59765625
- down_row: int32 [3072, 1], P('rows'), may hold values from 0 to 31; in each aligned block of 96 rows (0 to 95, 96 to 191, ...) at most 3 rows name the same one
- down_column: int32 [3072], P('rows'), may hold values from 0 to 63
- down_variant: int32 [3072], P('rows'), may hold values from 0 to 22
Outputs:
- screened: bfloat16 [384, 8192], P(('groups', 'rows'))
Inputs may be any that keep to these rules, and one draw needn't show every extreme that they name: `proj_column`: among the 96 gate and up blocks stored by one device, no hidden block is named more than 3 times, and in every draw some device names some hidden block exactly 3 times. `down_row`: among the 96 down blocks stored by one device, no hidden block is named more than 3 times, and in every draw some device names some hidden block exactly 3 times.
All inputs are finite; a program needn't handle non-finite values.
Results may differ from a plain program's by a relative error of at most 0.0051.
Values may be sent and summed in bfloat16 or wider, within the bound.
A program may use at most 128 MiB of HBM per device.

v0:
```python
import jax
import jax.numpy as jnp
from jax import lax
from jax.sharding import PartitionSpec as P

VARIANTS = 23


def slot_places(targets, capacity):
    slot_order = jnp.arange(targets.shape[0])
    earlier = (targets[:, None] == targets[None, :]) & (slot_order[None, :] < slot_order[:, None])
    slot_ranks = jnp.sum(earlier.astype(jnp.int32), axis=1)
    return targets * capacity + slot_ranks


def on_device(
    prompt,
    gate_weight,
    up_weight,
    down_weight,
    proj_blocks,
    proj_column,
    proj_row,
    proj_variant,
    proj_kind,
    down_blocks,
    down_row,
    down_column,
    down_variant,
):
    device_count = lax.axis_size("rows")
    block_size = proj_blocks.shape[1]
    tokens, model_width = prompt.shape
    width_blocks = model_width // block_size
    set_count = VARIANTS + 1
    proj_slots = proj_blocks.shape[0]
    down_slots = down_blocks.shape[0]
    proj_capacity = max(2, -(-proj_slots // device_count))
    down_capacity = max(2, -(-down_slots // device_count))
    proj_buffer = device_count * proj_capacity
    down_buffer = device_count * down_capacity
    prompt_blocks = prompt.reshape(tokens, width_blocks, block_size)
    proj_places = slot_places(proj_column[:, 0], proj_capacity)
    proj_ones = jnp.ones_like(proj_variant)
    send_blocks = (
        jnp.zeros((proj_buffer, block_size, block_size), proj_blocks.dtype)
        .at[proj_places]
        .set(proj_blocks)
    )
    send_meta = (
        jnp.zeros((proj_buffer, 4), jnp.int32)
        .at[proj_places]
        .set(jnp.stack([proj_row, proj_variant, proj_kind, proj_ones], axis=1))
    )
    got_blocks, got_meta = (
        lax.all_to_all(send_blocks, "rows", split_axis=0, concat_axis=0, tiled=True),
        lax.all_to_all(send_meta, "rows", split_axis=0, concat_axis=0, tiled=True),
    )
    chosen = jnp.take(prompt_blocks, got_meta[:, 0], axis=1)
    products = jnp.einsum("psd,sdf->spf", chosen, got_blocks, preferred_element_type=jnp.float32)
    meta_variant = got_meta[:, 1]
    meta_kind = got_meta[:, 2]
    meta_live = got_meta[:, 3]
    variant_ids = jnp.arange(VARIANTS)
    live_flags = meta_live.astype(jnp.float32)
    variant_pick = (meta_variant[:, None] == variant_ids[None, :]).astype(jnp.float32) * live_flags[
        :, None
    ]
    gate_pick = variant_pick * (meta_kind == 0).astype(jnp.float32)[:, None]
    up_pick = variant_pick * (meta_kind == 1).astype(jnp.float32)[:, None]
    gate_extra = jnp.einsum("sv,spf->vpf", gate_pick, products, precision=lax.Precision.HIGHEST)
    up_extra = jnp.einsum("sv,spf->vpf", up_pick, products, precision=lax.Precision.HIGHEST)
    gate_base = jnp.dot(prompt, gate_weight, preferred_element_type=jnp.float32)
    up_base = jnp.dot(prompt, up_weight, preferred_element_type=jnp.float32)
    zero_set = jnp.zeros((1, tokens, block_size), jnp.float32)
    gate_values = gate_base[None] + jnp.concatenate([zero_set, gate_extra], axis=0)
    up_values = up_base[None] + jnp.concatenate([zero_set, up_extra], axis=0)
    hidden = (jax.nn.silu(gate_values) * up_values).astype(jnp.bfloat16)
    down_places = slot_places(down_row[:, 0], down_capacity)
    down_ones = jnp.ones_like(down_variant)
    extra_term = jnp.zeros((set_count, tokens, width_blocks, block_size), jnp.float32)
    send_down = (
        jnp.zeros((down_buffer, block_size, block_size), down_blocks.dtype)
        .at[down_places]
        .set(down_blocks)
    )
    send_info = (
        jnp.zeros((down_buffer, 3), jnp.int32)
        .at[down_places]
        .set(jnp.stack([down_column, down_variant, down_ones], axis=1))
    )
    got_down, got_info = (
        lax.all_to_all(send_down, "rows", split_axis=0, concat_axis=0, tiled=True),
        lax.all_to_all(send_info, "rows", split_axis=0, concat_axis=0, tiled=True),
    )
    chosen_hidden = hidden[got_info[:, 1] + 1]
    corrections = jnp.einsum(
        "spf,sfd->spd", chosen_hidden, got_down, preferred_element_type=jnp.float32
    )
    corrections = corrections * got_info[:, 2].astype(jnp.float32)[:, None, None]
    extra_term = extra_term.at[got_info[:, 1] + 1, :, got_info[:, 0]].add(corrections)
    hidden_rows = hidden.reshape(set_count * tokens, block_size)
    extra_rows = extra_term.reshape(set_count * tokens, model_width)
    summed = lax.psum_scatter(
        jnp.dot(hidden_rows, down_weight, preferred_element_type=jnp.float32) + extra_rows,
        "rows",
        scatter_dimension=0,
        tiled=True,
    )
    return summed.astype(jnp.bfloat16)


def solution(mesh):
    in_specs = (
        P("groups", None),
        P(None, "rows"),
        P(None, "rows"),
        P("rows", None),
        P("rows", None, None),
        P("rows", None),
        P("rows"),
        P("rows"),
        P("rows"),
        P("rows", None, None),
        P("rows", None),
        P("rows"),
        P("rows"),
    )
    out_specs = P(("groups", "rows"), None)
    return jax.shard_map(
        on_device, mesh=mesh, in_specs=in_specs, out_specs=out_specs, check_vma=False
    )
```

profile of v0, /device:TPU:22, one launch (start us, length us, event | category | flops | bytes accessed | tf_op | source)
XLA Modules:
  0.0 512.6 jit_solution(5491425362117317955)
XLA Ops:
  4.2 5.9 %all-to-all-start.2 = ((s32[32,3,3]{1,2,0:T(4,128)}), s32[32,3,3]{1,2,0:T(4,128)S(1)}, u32[]{:S(2)}, u32[]{:S(2)}) async-start(s32[32,3,3]{1,2,0:T(4,128)} %copy.61), calls=%async_computation.2 | async-start | bytes 131072 | tf_op jit(solution)/shard_map/all_to_all | solution.py:94
  14.2 5.8 %all-to-all-start = ((s32[32,3,4]{1,2,0:T(4,128)}), s32[32,3,4]{1,2,0:T(4,128)S(1)}, u32[]{:S(2)}, u32[]{:S(2)}) async-start(s32[32,3,4]{1,2,0:T(4,128)} %copy.53), calls=%async_computation | async-start | bytes 131072 | tf_op jit(solution)/shard_map/all_to_all | solution.py:57
  20.1 2.5 broadcast.55.clone
  22.5 14.8 %scatter_fusion = bf16[96,128,128]{2,1,0:T(8,128)(2,1)} fusion(bf16[96,128,128]{2,1,0:T(8,128)(2,1)} %broadcast.55.clone, s32[96]{0:T(128)S(1)} %fusion.31, bf16[96,128,128]{2,1,0:T(8,128)(2,1)} %param.17), kind=kCustom, calls=%fused_computation.3 | custom fusion | bytes 9437568 | tf_op jit(solution)/shard_map/scatter | solution.py:48
  37.4 5.9 %all-to-all-start.1 = ((bf16[96,128,128]{2,1,0:T(8,128)(2,1)}), bf16[96,128,128]{2,1,0:T(8,128)(2,1)}, u32[]{:S(2)}, u32[]{:S(2)}) async-start(bf16[96,128,128]{2,1,0:T(8,128)(2,1)} %scatter_fusion), calls=%async_computation.1 | async-start | bytes 6291456 | tf_op jit(solution)/shard_map/all_to_all | solution.py:56
  43.2 2.5 broadcast.55.clone.1
  45.7 14.8 %scatter_fusion.1 = bf16[96,128,128]{2,1,0:T(8,128)(2,1)} fusion(bf16[96,128,128]{2,1,0:T(8,128)(2,1)} %broadcast.55.clone.1, s32[96]{0:T(128)S(1)} %fusion.32, bf16[96,128,128]{2,1,0:T(8,128)(2,1)} %param.22), kind=kCustom, calls=%fused_computation.5 | custom fusion | bytes 9437568 | tf_op jit(solution)/shard_map/scatter | solution.py:85
  60.5 50.8 %all-to-all-done.1 = bf16[96,128,128]{2,1,0:T(8,128)(2,1)} async-done(((bf16[96,128,128]{2,1,0:T(8,128)(2,1)}), bf16[96,128,128]{2,1,0:T(8,128)(2,1)}, u32[]{:S(2)}, u32[]{:S(2)}) %all-to-all-start.1) | async-done | bytes 3145760 | tf_op jit(solution)/shard_map/all_to_all | solution.py:56
  111.4 7.3 %all-to-all-start.3 = ((bf16[96,128,128]{2,1,0:T(8,128)(2,1)}), bf16[96,128,128]{2,1,0:T(8,128)(2,1)}, u32[]{:S(2)}, u32[]{:S(2)}) async-start(bf16[96,128,128]{2,1,0:T(8,128)(2,1)} %scatter_fusion.1), calls=%async_computation.3 | async-start | bytes 6291456 | tf_op jit(solution)/shard_map/all_to_all | solution.py:93
  118.8 2.0 fusion.40
  120.8 2.0 fusion.41
  123.8 2.9 fusion.5
  128.8 58.1 %all-to-all-done.3 = bf16[96,128,128]{2,1,0:T(8,128)(2,1)} async-done(((bf16[96,128,128]{2,1,0:T(8,128)(2,1)}), bf16[96,128,128]{2,1,0:T(8,128)(2,1)}, u32[]{:S(2)}, u32[]{:S(2)}) %all-to-all-start.3) | async-done | bytes 3145760 | tf_op jit(solution)/shard_map/all_to_all | solution.py:93
  186.9 2.8 convolution_multiply_fusion
  189.7 5.9 %broadcast_in_dim.19 = f32[24,16,64,128]{3,1,2,0:T(8,128)} broadcast(f32[]{:T(128)} %constant.15.clone.1), dimensions={} | broadcast | bytes 12582916 | tf_op jit(solution)/shard_map/broadcast_in_dim | solution.py:81
  195.6 11.2 %scatter_fusion.2 = f32[24,16,64,128]{3,1,2,0:T(8,128)} fusion(f32[24,16,64,128]{3,1,2,0:T(8,128)} %broadcast_in_dim.19, s32[96]{0:T(128)S(1)} %get-tuple-element.13, f32[96,16,128]{2,1,0:T(8,128)S(1)} %convolution_multiply_fusion), kind=kCustom, calls=%fused_computation.6 | custom fusion | flops 196608 | bytes 2360064 | tf_op jit(solution)/shard_map/scatter-add | solution.py:101
  206.8 13.9 %copy.64 = f32[24,16,64,128]{3,2,1,0:T(8,128)} copy(f32[24,16,64,128]{3,1,2,0:T(8,128)} %scatter_fusion.2) | data formatting | bytes 25165824 | tf_op jit(solution)/shard_map/scatter-add | solution.py:101
  220.6 17.2 %bitcast_add_fusion = f32[384,8192]{1,0:T(8,128)} fusion(f32[48,8,64,128]{3,2,1,0:T(8,128)} %bitcast.71, bf16[384,128]{1,0:T(8,128)(2,1)S(1)} %bitcast.72, bf16[128,8192]{1,0:T(8,128)(2,1)S(1)} %copy-done), kind=kOutput, calls=%fused_computation.7 | convolution fusion | flops 808452096 | bytes 27361280 | tf_op jit(solution)/shard_map/dot_general | solution.py:105
  237.8 184.1 %fusion = f32[16,8192]{1,0:T(8,128)S(1)} fusion(f32[384,8192]{1,0:T(8,128)} %bitcast_add_fusion), kind=kCustom, calls=%all-reduce-scatter | all-reduce-scatter fusion | flops 4194305 | bytes 13107200
  421.9 1.9 collective-permute-start
  423.9 1.9 collective-permute-start.1
  425.9 4.0 collective-permute-start.7
  429.9 1.9 collective-permute-start.2
  431.8 4.5 collective-permute-start.3
  436.3 3.8 collective-permute-done.7
  442.1 2.2 collective-permute-start.5
  444.3 1.9 collective-permute-start.6
  446.2 3.1 collective-permute-done.3
  449.3 5.6 %collective-permute-done.4 = bf16[16,8192]{1,0:T(8,128)(2,1)} collective-permute-done((bf16[16,8192]{1,0:T(8,128)(2,1)S(1)}, bf16[16,8192]{1,0:T(8,128)(2,1)}, u32[]{:S(2)}, u32[]{:S(2)}) %collective-permute-start.4) | collective-permute-done | bytes 262176
  454.9 5.6 %collective-permute-done.5 = bf16[16,8192]{1,0:T(8,128)(2,1)} collective-permute-done((bf16[16,8192]{1,0:T(8,128)(2,1)S(1)}, bf16[16,8192]{1,0:T(8,128)(2,1)}, u32[]{:S(2)}, u32[]{:S(2)}) %collective-permute-start.5) | collective-permute-done | bytes 262176
  460.6 15.6 %collective-permute-done.6 = bf16[16,8192]{1,0:T(8,128)(2,1)} collective-permute-done((bf16[16,8192]{1,0:T(8,128)(2,1)S(1)}, bf16[16,8192]{1,0:T(8,128)(2,1)}, u32[]{:S(2)}, u32[]{:S(2)}) %collective-permute-start.6) | collective-permute-done | bytes 262176
  476.2 34.6 %concatenate.14 = bf16[140,8192]{1,0:T(8,128)(2,1)} concatenate(bf16[12,8192]{1,0:T(8,128)(2,1)} %copy-done.2, bf16[16,8192]{1,0:T(8,128)(2,1)} %collective-permute-done.6, bf16[16,8192]{1,0:T(8,128)(2,1)} %collective-permute-done.5, bf16[16,8192]{1,0:T(8,128)(2,1)} %collective-permute-done.4, bf16[16,8192]{1,0:T(8,128)(2,1)} %collective-permute-done.3, ...), dimensions={0} | concatenate | bytes 4849664
  (47 shorter events, 15.2 us)
Async XLA Ops:
  0.0 220.6 %copy-start = (bf16[128,8192]{1,0:T(8,128)(2,1)S(1)}, bf16[128,8192]{1,0:T(8,128)(2,1)}, u32[]{:S(2)}) copy-start(bf16[128,8192]{1,0:T(8,128)(2,1)} %param.16) | copy-start | bytes 6291460
  4.2 10.0 %all-to-all-start.2 = ((s32[32,3,3]{1,2,0:T(4,128)}), s32[32,3,3]{1,2,0:T(4,128)S(1)}, u32[]{:S(2)}, u32[]{:S(2)}) async-start(s32[32,3,3]{1,2,0:T(4,128)} %copy.61), calls=%async_computation.2 | async-start | bytes 131072 | tf_op jit(solution)/shard_map/all_to_all | solution.py:94
  14.2 23.1 %all-to-all-start = ((s32[32,3,4]{1,2,0:T(4,128)}), s32[32,3,4]{1,2,0:T(4,128)S(1)}, u32[]{:S(2)}, u32[]{:S(2)}) async-start(s32[32,3,4]{1,2,0:T(4,128)} %copy.53), calls=%async_computation | async-start | bytes 131072 | tf_op jit(solution)/shard_map/all_to_all | solution.py:57
  37.4 74.0 %all-to-all-start.1 = ((bf16[96,128,128]{2,1,0:T(8,128)(2,1)}), bf16[96,128,128]{2,1,0:T(8,128)(2,1)}, u32[]{:S(2)}, u32[]{:S(2)}) async-start(bf16[96,128,128]{2,1,0:T(8,128)(2,1)} %scatter_fusion), calls=%async_computation.1 | async-start | bytes 6291456 | tf_op jit(solution)/shard_map/all_to_all | solution.py:56
  60.5 58.2 %copy-start.1 = (bf16[16,8192]{1,0:T(8,128)(2,1)S(1)}, bf16[16,8192]{1,0:T(8,128)(2,1)}, u32[]{:S(2)}) copy-start(bf16[16,8192]{1,0:T(8,128)(2,1)} %param.13) | copy-start | bytes 786436
  111.4 75.5 %all-to-all-start.3 = ((bf16[96,128,128]{2,1,0:T(8,128)(2,1)}), bf16[96,128,128]{2,1,0:T(8,128)(2,1)}, u32[]{:S(2)}, u32[]{:S(2)}) async-start(bf16[96,128,128]{2,1,0:T(8,128)(2,1)} %scatter_fusion.1), calls=%async_computation.3 | async-start | bytes 6291456 | tf_op jit(solution)/shard_map/all_to_all | solution.py:93
  421.9 20.1 %collective-permute-start = (bf16[16,8192]{1,0:T(8,128)(2,1)S(1)}, bf16[16,8192]{1,0:T(8,128)(2,1)S(1)}, u32[]{:S(2)}, u32[]{:S(2)}) collective-permute-start(bf16[16,8192]{1,0:T(8,128)(2,1)S(1)} %convert.18), channel_id=1, source_target_pairs={{0,1},{1,2},{2,3},{3,4},{4,5},{5,6},{6,7},{7,8},{8,9},{9,10},{10,1... | collective-permute-start | bytes 786440
  423.9 20.4 %collective-permute-start.1 = (bf16[16,8192]{1,0:T(8,128)(2,1)S(1)}, bf16[16,8192]{1,0:T(8,128)(2,1)S(1)}, u32[]{:S(2)}, u32[]{:S(2)}) collective-permute-start(bf16[16,8192]{1,0:T(8,128)(2,1)S(1)} %convert.18), channel_id=1, source_target_pairs={{0,2},{1,3},{2,4},{3,5},{4,6},{5,7},{6,8},{7,9},{8,10},{9,11},{10,... | collective-permute-start | bytes 786440
  425.9 14.3 %collective-permute-start.7 = (bf16[12,8192]{1,0:T(8,128)(2,1)S(1)}, bf16[12,8192]{1,0:T(8,128)(2,1)S(1)}, u32[]{:S(2)}, u32[]{:S(2)}) collective-permute-start(bf16[12,8192]{1,0:T(8,128)(2,1)S(1)} %slice.35), channel_id=1, source_target_pairs={{0,8},{1,9},{2,10},{3,11},{4,12},{5,13},{6,14},{7,15},{8,16},{9,17... | collective-permute-start | bytes 589832
  429.9 16.4 %collective-permute-start.2 = (bf16[16,8192]{1,0:T(8,128)(2,1)S(1)}, bf16[16,8192]{1,0:T(8,128)(2,1)}, u32[]{:S(2)}, u32[]{:S(2)}) collective-permute-start(bf16[16,8192]{1,0:T(8,128)(2,1)S(1)} %convert.18), channel_id=1, source_target_pairs={{0,3},{1,4},{2,5},{3,6},{4,7},{5,8},{6,9},{7,10},{8,11},{9,12},{10... | collective-permute-start | bytes 786440
  431.8 17.6 %collective-permute-start.3 = (bf16[16,8192]{1,0:T(8,128)(2,1)S(1)}, bf16[16,8192]{1,0:T(8,128)(2,1)}, u32[]{:S(2)}, u32[]{:S(2)}) collective-permute-start(bf16[16,8192]{1,0:T(8,128)(2,1)S(1)} %convert.18), channel_id=1, source_target_pairs={{0,4},{1,5},{2,6},{3,7},{4,8},{5,9},{6,10},{7,11},{8,12},{9,13},{1... | collective-permute-start | bytes 786440
  440.1 6.1 %copy-start.2 = (bf16[12,8192]{1,0:T(8,128)(2,1)}, bf16[12,8192]{1,0:T(8,128)(2,1)S(1)}, u32[]{:S(2)}) copy-start(bf16[12,8192]{1,0:T(8,128)(2,1)S(1)} %collective-permute-done.7) | copy-start | bytes 589828
  440.1 14.8 %collective-permute-start.4 = (bf16[16,8192]{1,0:T(8,128)(2,1)S(1)}, bf16[16,8192]{1,0:T(8,128)(2,1)}, u32[]{:S(2)}, u32[]{:S(2)}) collective-permute-start(bf16[16,8192]{1,0:T(8,128)(2,1)S(1)} %convert.18), channel_id=1, source_target_pairs={{0,5},{1,6},{2,7},{3,8},{4,9},{5,10},{6,11},{7,12},{8,13},{9,14},{... | collective-permute-start | bytes 786440
  442.1 18.5 %collective-permute-start.5 = (bf16[16,8192]{1,0:T(8,128)(2,1)S(1)}, bf16[16,8192]{1,0:T(8,128)(2,1)}, u32[]{:S(2)}, u32[]{:S(2)}) collective-permute-start(bf16[16,8192]{1,0:T(8,128)(2,1)S(1)} %convert.18), channel_id=1, source_target_pairs={{0,6},{1,7},{2,8},{3,9},{4,10},{5,11},{6,12},{7,13},{8,14},{9,15},... | collective-permute-start | bytes 786440
  444.3 31.9 %collective-permute-start.6 = (bf16[16,8192]{1,0:T(8,128)(2,1)S(1)}, bf16[16,8192]{1,0:T(8,128)(2,1)}, u32[]{:S(2)}, u32[]{:S(2)}) collective-permute-start(bf16[16,8192]{1,0:T(8,128)(2,1)S(1)} %convert.18), channel_id=1, source_target_pairs={{0,7},{1,8},{2,9},{3,10},{4,11},{5,12},{6,13},{7,14},{8,15},{9,16}... | collective-permute-start | bytes 786440
where the time goes:
time: 516 us; the launch traced here: 513 us
  blocking collectives  184 us (36%)
  waiting for transfers between devices  143 us (28%)
  local copies, waits for them, and re-layouts  96 us (19%)
  starting transfers between devices  45.2 us (9%)
  matrix products  28.2 us (5%)
  other arithmetic  16 us (3%)
    unnamed x1, blocking collectives  184 us
    all_to_all x1, waiting for transfers between devices, on_device(): lax.all_to_all(send_down, 'rows', split_axis=0, concat_axis=0, tiled=True)  58.1 us
    all_to_all x1, waiting for transfers between devices, on_device(): lax.all_to_all(send_blocks, 'rows', split_axis=0, concat_axis=0, tiled=True)  50.8 us
    unnamed x8, local copies, waits for them, and re-layouts  34.7 us
    unnamed x8, waiting for transfers between devices  33.7 us
    unnamed x8, starting transfers between devices  20.3 us
    dot_general x1, matrix products, on_device(): jnp.dot(hidden_rows, down_weight, preferred_element_type=jnp.float32)  17.2 us
    scatter x1, local copies, waits for them, and re-layouts, on_device(): send_blocks = jnp.zeros((proj_buffer, block_size, block_size), proj_block...  14.8 us
  transfers between devices with their start and end apart: 12, of which 7 were waited for; matrix products, arithmetic and copies ran while one was open for 9% of the time, Pallas kernels for 0%

commit v1 on v0

v1 whole, which is shorter than its diff:
```python
import functools

import jax
import jax.numpy as jnp
from jax import lax
from jax.experimental import pallas as pl
from jax.experimental.pallas import tpu as pltpu
from jax.sharding import PartitionSpec as P

VARIANTS = 23
UNIT_ROWS = 48
LANES = 4
VMEM_LIMIT = 56 * 1024 * 1024


def slot_places(targets, capacity):
    order = jnp.arange(targets.shape[0])
    earlier = (targets[:, None] == targets[None, :]) & (order[None, :] < order[:, None])
    return targets * capacity + jnp.sum(earlier.astype(jnp.int32), axis=1)


def down_kernel(device_count, row_ref, column_ref, variant_ref, all_ref, own_ref, weight_ref, block_ref, out_ref, acc):
    total_rows, model_width = acc.shape
    tile = 1024

    def dense(step, _):
        columns = pl.ds(pl.multiple_of(step * tile, tile), tile)
        acc[:, columns] = jnp.dot(own_ref[...], weight_ref[:, columns], preferred_element_type=jnp.float32)
        return 0

    lax.fori_loop(0, model_width // tile, dense, 0)
    slots = block_ref.shape[0]
    batch = 8

    def correct(step, _):
        parts = []
        for i in range(batch):
            j = step * batch + i
            first = pl.multiple_of((variant_ref[j] + 1) * 16, 16)
            rows = all_ref[row_ref[j], pl.ds(first, 16), :]
            parts.append((j, first, jnp.dot(rows, block_ref[j], preferred_element_type=jnp.float32)))
        for j, first, part in parts:
            columns = pl.ds(pl.multiple_of(column_ref[j] * 128, 128), 128)
            acc[pl.ds(first, 16), columns] += part
        return 0

    lax.fori_loop(0, slots // batch, correct, 0)
    own_rows = total_rows // device_count
    pieces = UNIT_ROWS // own_rows
    width = model_width // pieces
    narrow = width // LANES
    owners = 24 // own_rows

    def pack(step, _):
        first = pl.multiple_of(step * 24, 24)
        for owner in range(owners):
            place = step * (owners // 2) + owner // 2
            for channel in range(LANES):
                low = channel * narrow
                parts = [
                    acc[pl.ds(first, 24), piece * width + low : piece * width + low + narrow][
                        owner * own_rows : (owner + 1) * own_rows
                    ]
                    for piece in range(pieces)
                ]
                out_ref[channel, owner % 2, place] = jnp.concatenate(parts, axis=0).astype(jnp.bfloat16)
        return 0

    lax.fori_loop(0, total_rows // 24, pack, 0)


def down_partial(device_count, row, column, variant, gathered, own, weight, blocks):
    total_rows = own.shape[0]
    model_width = weight.shape[1]
    width = model_width * (total_rows // device_count) // UNIT_ROWS
    return pl.pallas_call(
        functools.partial(down_kernel, device_count),
        out_shape=jax.ShapeDtypeStruct(
            (LANES, 2, device_count // 2, UNIT_ROWS, width // LANES), jnp.bfloat16
        ),
        in_specs=[pl.BlockSpec(memory_space=pltpu.SMEM)] * 3 + [pl.BlockSpec(memory_space=pltpu.VMEM)] * 4,
        out_specs=pl.BlockSpec(memory_space=pltpu.VMEM),
        scratch_shapes=[pltpu.VMEM((total_rows, model_width), jnp.float32)],
        compiler_params=pltpu.CompilerParams(vmem_limit_bytes=VMEM_LIMIT),
    )(row, column, variant, gathered, own, weight, blocks)


def bit_orders(device_count):
    if device_count == 32:
        return [[0, 1, 2, 3, 4], [0, 2, 1, 3, 4]]
    bits = device_count.bit_length() - 1
    middle = (bits + 1) // 2
    first, second = list(range(1, middle)), list(range(middle, bits))
    return [[0] + first + second, [0] + second + first]


def scatter_kernel(device_count, part_ref, out_ref, *scratch):
    stages = device_count.bit_length() - 1
    received = scratch[:stages]
    sending = (None,) + scratch[stages : 2 * stages - 1]
    kept = (None,) + scratch[2 * stages - 1 : 3 * stages - 2]
    send_sem, recv_sem = scratch[3 * stages - 2 :]
    me = lax.axis_index("rows")
    half = device_count // 2
    orders = [bit_orders(device_count)[c % 2] for c in range(LANES)]
    my_bits = [(me // (1 << b)) % 2 for b in range(stages)]
    partners = [me + (1 - 2 * my_bits[b]) * (1 << b) for b in range(stages)]

    barrier = pltpu.get_barrier_semaphore()
    for b in range(stages):
        pl.semaphore_signal(barrier, inc=1, device_id={"rows": partners[b]}, device_id_type=pl.DeviceIdType.MESH)
    pl.semaphore_wait(barrier, stages)

    def transfer(channel, stage):
        source = part_ref.at[channel, 1 - my_bits[0]] if stage == 0 else sending[stage].at[channel]
        return pltpu.make_async_remote_copy(
            src_ref=source,
            dst_ref=received[stage].at[channel],
            send_sem=send_sem.at[channel, stage],
            recv_sem=recv_sem.at[channel, stage],
            device_id={"rows": partners[orders[channel][stage]]},
            device_id_type=pl.DeviceIdType.MESH,
        )

    copies = {}
    for channel in range(LANES):
        copies[channel, 0] = transfer(channel, 0)
        copies[channel, 0].start()
    for stage in range(stages):
        count = half >> stage
        for channel in range(LANES):
            copies[channel, stage].wait_recv()

            def value(i):
                if stage == 0:
                    mine = part_ref[channel, my_bits[0], i].astype(jnp.float32)
                else:
                    mine = kept[stage][channel, i]
                return mine + received[stage][channel, i].astype(jnp.float32)

            if stage == stages - 1:
                out_ref[channel] = value(0).astype(jnp.bfloat16)
                continue
            bit = orders[channel][stage + 1]
            low = 1 << sum(1 for other in orders[channel][stage + 2 :] if other < bit)

            def pick(j, side):
                return (j // low) * (2 * low) + side * low + j % low

            def send_side(j, _):
                sending[stage + 1][channel, j] = value(pick(j, 1 - my_bits[bit])).astype(jnp.bfloat16)
                return 0

            def keep_side(j, _):
                kept[stage + 1][channel, j] = value(pick(j, my_bits[bit]))
                return 0

            lax.fori_loop(0, count // 2, send_side, 0)
            copies[channel, stage + 1] = transfer(channel, stage + 1)
            copies[channel, stage + 1].start()
            lax.fori_loop(0, count // 2, keep_side, 0)
    for copy in copies.values():
        copy.wait_send()


def reduce_scatter(device_count, part):
    narrow = part.shape[-1]
    stages = device_count.bit_length() - 1
    half = device_count // 2
    counts = [half >> s for s in range(stages)]
    scratch = [pltpu.VMEM((LANES, k, UNIT_ROWS, narrow), jnp.bfloat16) for k in counts]
    scratch += [pltpu.VMEM((LANES, k, UNIT_ROWS, narrow), jnp.bfloat16) for k in counts[1:]]
    scratch += [pltpu.VMEM((LANES, k, UNIT_ROWS, narrow), jnp.float32) for k in counts[1:]]
    scratch += [pltpu.SemaphoreType.DMA((LANES, stages))] * 2
    return pl.pallas_call(
        functools.partial(scatter_kernel, device_count),
        out_shape=jax.ShapeDtypeStruct((LANES, UNIT_ROWS, narrow), jnp.bfloat16),
        in_specs=[pl.BlockSpec(memory_space=pltpu.VMEM)],
        out_specs=pl.BlockSpec(memory_space=pltpu.VMEM),
        scratch_shapes=scratch,
        compiler_params=pltpu.CompilerParams(
            collective_id=0, has_side_effects=True, vmem_limit_bytes=VMEM_LIMIT
        ),
    )(part)


def on_device(
    prompt,
    gate_weight,
    up_weight,
    down_weight,
    proj_blocks,
    proj_column,
    proj_row,
    proj_variant,
    proj_kind,
    down_blocks,
    down_row,
    down_column,
    down_variant,
):
    device_count = lax.axis_size("rows")
    block_size = proj_blocks.shape[1]
    tokens, model_width = prompt.shape
    width_blocks = model_width // block_size
    set_count = VARIANTS + 1
    slots = proj_blocks.shape[0]
    capacity = max(2, -(-slots // device_count))
    places = device_count * capacity

    prompt_blocks = prompt.reshape(tokens, width_blocks, block_size).transpose(1, 0, 2)
    chosen = jnp.take(prompt_blocks, proj_row, axis=0)
    products = jnp.einsum("spd,sdf->spf", chosen, proj_blocks, preferred_element_type=jnp.float32)
    codes = (proj_variant * 2 + proj_kind + 2).astype(jnp.bfloat16)
    payload = jnp.concatenate(
        [
            products.astype(jnp.bfloat16).reshape(slots, tokens * block_size),
            jnp.broadcast_to(codes[:, None], (slots, block_size)),
        ],
        axis=1,
    )
    place_of = slot_places(proj_column[:, 0], capacity)
    spread = (jnp.arange(places)[:, None] == place_of[None, :]).astype(jnp.bfloat16)
    sent = jnp.dot(spread, payload, preferred_element_type=jnp.float32).astype(jnp.bfloat16)
    got = lax.all_to_all(sent, "rows", split_axis=0, concat_axis=0, tiled=True)
    got_codes = got[:, tokens * block_size].astype(jnp.int32)
    values = got[:, : tokens * block_size]
    pick = (got_codes[None, :] == jnp.arange(2 * set_count)[:, None]).astype(jnp.bfloat16)
    pick = pick * (jnp.arange(2 * set_count)[:, None] >= 2).astype(jnp.bfloat16)
    extra = jnp.dot(pick, values, preferred_element_type=jnp.float32)
    extra = extra.reshape(set_count, 2, tokens, block_size)
    gate_base = jnp.dot(prompt, gate_weight, preferred_element_type=jnp.float32)
    up_base = jnp.dot(prompt, up_weight, preferred_element_type=jnp.float32)
    gate_values = gate_base[None] + extra[:, 0]
    up_values = up_base[None] + extra[:, 1]
    hidden = (jax.nn.silu(gate_values) * up_values).astype(jnp.bfloat16)
    hidden = hidden.reshape(set_count * tokens, block_size)
    gathered = lax.all_gather(hidden, "rows", axis=0, tiled=False)
    part = down_partial(
        device_count, down_row[:, 0], down_column, down_variant, gathered, hidden, down_weight, down_blocks
    )
    chunk = reduce_scatter(device_count, part)
    own_rows = set_count * tokens // device_count
    pieces = UNIT_ROWS // own_rows
    narrow = chunk.shape[-1]
    chunk = chunk.reshape(LANES, pieces, own_rows, narrow).transpose(2, 1, 0, 3)
    return chunk.reshape(own_rows, model_width)


def solution(mesh):
    in_specs = (
        P("groups", None),
        P(None, "rows"),
        P(None, "rows"),
        P("rows", None),
        P("rows", None, None),
        P("rows", None),
        P("rows"),
        P("rows"),
        P("rows"),
        P("rows", None, None),
        P("rows", None),
        P("rows"),
        P("rows"),
    )
    return jax.shard_map(
        on_device, mesh=mesh, in_specs=in_specs, out_specs=P(("groups", "rows"), None), check_vma=False
    )
```

time: 516 us -> 173 us (0.34)
  the two profiles are of different devices: /device:TPU:22 before, /device:TPU:0 now
where the time goes in v1:
time: 173 us; the launch traced here: 172 us
  waiting for transfers between devices  70.4 us (41%)
  Pallas kernels  59.4 us (34%)
  between operations  13.6 us (8%)
  local copies, waits for them, and re-layouts  8.93 us (5%)
  starting transfers between devices  7.45 us (4%)
  matrix products  6.78 us (4%)
  other arithmetic  5.49 us (3%)
    all_gather x1, waiting for transfers between devices, on_device(): gathered = lax.all_gather(hidden, 'rows', axis=0, tiled=False)  57 us
    pallas_call x1, Pallas kernels, reduce_scatter(): pl.pallas_call(functools.partial(scatter_kernel, device_count), out_shape...  47.3 us
    all_to_all x1, waiting for transfers between devices, on_device(): got = lax.all_to_all(sent, 'rows', split_axis=0, concat_axis=0, tiled=True)  13.5 us
    pallas_call x1, Pallas kernels, down_partial(): pl.pallas_call(functools.partial(down_kernel, device_count), out_shape=ja...  12.1 us
    all_to_all x1, starting transfers between devices, on_device(): got = lax.all_to_all(sent, 'rows', split_axis=0, concat_axis=0, tiled=True)  7.41 us
    all_to_all x2, local copies, waits for them, and re-layouts, on_device(): got = lax.all_to_all(sent, 'rows', split_axis=0, concat_axis=0, tiled=True)  4.16 us
  transfers between devices with their start and end apart: 2, of which 2 were waited for; matrix products, arithmetic and copies ran while one was open for 2% of the time, Pallas kernels for 0%

profile of v1, /device:TPU:0, one launch (start us, length us, event | category | flops | bytes accessed | tf_op | source)
XLA Modules:
  0.0 172.1 jit_solution(12076011593179449295)
XLA Ops:
  6.5 0.8 compare_and_fusion
  7.3 0.8 compare_select_fusion
  8.2 0.9 convert_reduce_fusion.1
  9.1 0.7 multiply_add_fusion
  9.7 1.0 bitcast_bitcast_fusion
  10.7 1.4 gather_fusion
  12.1 2.0 %convolution_convert_fusion.1 = bf16[96,16,128]{2,1,0:T(8,128)(2,1)S(1)} fusion(bf16[96,128,128]{2,1,0:T(8,128)(2,1)S(1)} %copy-done, bf16[96,16,128]{2,1,0:T(8,128)(2,1)} %gather_fusion, pred[96]{0:T(512)(128)(4,1)S(1)} %compare_and_fusion), kind=kOutput, calls=%fused_computation.2 | convolution fusion | flops 50724864 | bytes 3932256 | tf_op jit(solution)/shard_map/spd,sdf->spf/dot_general | solution.py:213
  14.1 0.0 copy-start.1
  14.2 0.1 copy.43
  14.3 0.1 broadcast_in_dim.17
  14.4 1.0 convolution_convert_fusion
  15.4 2.1 %all_to_all.8 = bf16[32,3,2176]{2,1,0:T(4,128)(2,1)} reshape(bf16[96,2176]{1,0:T(8,128)(2,1)} %convolution_convert_fusion) | data formatting | bytes 835584 | tf_op jit(solution)/shard_map/all_to_all | solution.py:225
  17.5 7.4 %all-to-all-start = ((bf16[32,3,2176]{2,1,0:T(4,128)(2,1)}), bf16[32,3,2176]{2,1,0:T(4,128)(2,1)}, u32[]{:S(2)}, u32[]{:S(2)}) async-start(bf16[32,3,2176]{2,1,0:T(4,128)(2,1)} %all_to_all.8), calls=%async_computation | async-start | bytes 1114112 | tf_op jit(solution)/shard_map/all_to_all | solution.py:225
  24.9 0.0 all-gather.2.cloned.1.call-start
  25.0 0.0 copy-start.2
  25.0 2.1 %fusion.22 = f32[16,128]{1,0:T(8,128)S(1)} fusion(bf16[16,8192]{1,0:T(8,128)(2,1)S(1)} %copy-done.1, bf16[8192,128]{1,0:T(8,128)(2,1)} %param.14), kind=kOutput, calls=%fused_computation.42 | convolution fusion | flops 33554432 | bytes 2367488 | tf_op jit(solution)/shard_map/dot_general | solution.py:232
  27.1 0.1 copy-done.2
  27.2 0.4 fusion.23
  27.6 13.5 %all-to-all-done = bf16[32,3,2176]{2,1,0:T(4,128)(2,1)} async-done(((bf16[32,3,2176]{2,1,0:T(4,128)(2,1)}), bf16[32,3,2176]{2,1,0:T(4,128)(2,1)}, u32[]{:S(2)}, u32[]{:S(2)}) %all-to-all-start) | async-done | bytes 417824 | tf_op jit(solution)/shard_map/all_to_all | solution.py:225
  41.1 2.1 %all_to_all.10 = bf16[96,2176]{1,0:T(8,128)(2,1)} reshape(bf16[32,3,2176]{2,1,0:T(4,128)(2,1)} %all-to-all-done) | data formatting | bytes 835584 | tf_op jit(solution)/shard_map/all_to_all | solution.py:225
  43.1 0.8 convert_reduce_fusion
  44.0 1.2 convolution_bitcast_fusion
  45.2 0.1 copy.40
  45.4 0.7 fusion.9
  46.1 0.0 all-gather.2.cloned.1.call-update
  46.1 0.7 fusion.7.own_ref
  46.8 57.0 %all-gather.2.cloned.1.call-done.all_ref = bf16[32,384,128]{2,1,0:T(8,128)(2,1)} async-done(((bf16[1,384,128]{2,1,0:T(8,128)(2,1)}), bf16[32,384,128]{2,1,0:T(8,128)(2,1)}) %all-gather.2.cloned.1.call-update) | async-done | bytes 3145744 | tf_op jit(solution)/shard_map/all_gather | solution.py:238
  103.8 12.1 %shard_map.127.part_ref = bf16[4,2,16,48,512]{4,3,2,1,0:T(8,128)(2,1)} custom-call(s32[96]{0:T(128)} %bitcast.70, s32[96]{0:T(128)} %column_ref.1, s32[96]{0:T(128)} %variant_ref.1, bf16[32,384,128]{2,1,0:T(8,128)(2,1)} %all-gather.2.cloned.1.call-done.all_ref, bf16[384,128]{1,0:T(8,128)(2,1)} %fusion.7.own_ref, bf16[128,8192]{1,0:T(8,128)(2,1)} %weight_ref.1, ...), custom_call_target="tpu_custom_call" | custom-call | tf_op jit(solution)/shard_map/pallas_call | solution.py:76
  115.9 47.3 %shard_map.128 = bf16[4,48,512]{2,1,0:T(8,128)(2,1)} custom-call(bf16[4,2,16,48,512]{4,3,2,1,0:T(8,128)(2,1)} %shard_map.127.part_ref), custom_call_target="tpu_custom_call" | custom-call | tf_op jit(solution)/shard_map/pallas_call | solution.py:175
  163.3 1.1 copy.34
  164.3 0.1 copy.35
  164.4 0.8 reshape.116
  (13 shorter events, 0.1 us)
Async XLA Ops:
  6.5 5.6 %copy-start = (bf16[96,128,128]{2,1,0:T(8,128)(2,1)S(1)}, bf16[96,128,128]{2,1,0:T(8,128)(2,1)}, u32[]{:S(2)}) copy-start(bf16[96,128,128]{2,1,0:T(8,128)(2,1)} %param.17) | copy-start | bytes 9437188
  12.1 2.1 %copy-start.3 = (s32[96]{0:T(128)S(1)}, s32[96]{0:T(128)}, u32[]{:S(2)}) copy-start(s32[96]{0:T(128)} %param.21) | copy-start | bytes 1156
  12.1 2.1 %copy-start.4 = (s32[96]{0:T(128)S(1)}, s32[96]{0:T(128)}, u32[]{:S(2)}) copy-start(s32[96]{0:T(128)} %param.20) | copy-start | bytes 1156
  14.1 10.9 %copy-start.1 = (bf16[16,8192]{1,0:T(8,128)(2,1)S(1)}, bf16[16,8192]{1,0:T(8,128)(2,1)}, u32[]{:S(2)}) copy-start(bf16[16,8192]{1,0:T(8,128)(2,1)} %param.13) | copy-start | bytes 786436
  17.5 23.5 %all-to-all-start = ((bf16[32,3,2176]{2,1,0:T(4,128)(2,1)}), bf16[32,3,2176]{2,1,0:T(4,128)(2,1)}, u32[]{:S(2)}, u32[]{:S(2)}) async-start(bf16[32,3,2176]{2,1,0:T(4,128)(2,1)} %all_to_all.8), calls=%async_computation | async-start | bytes 1114112 | tf_op jit(solution)/shard_map/all_to_all | solution.py:225
  24.9 78.9 %all-gather.2.cloned.1.call-start = ((), (), s32[]{:S(2)}) async-start(), calls=%async_computation.1 | async-start | bytes 3244032 | tf_op jit(solution)/shard_map/all_gather | solution.py:238
  25.0 2.2 %copy-start.2 = (bf16[8192,128]{1,0:T(8,128)(2,1)S(1)}, bf16[8192,128]{1,0:T(8,128)(2,1)}, u32[]{:S(2)}) copy-start(bf16[8192,128]{1,0:T(8,128)(2,1)} %param.15) | copy-start | bytes 6291460
Sparse Core Ops, SparseCore 0:
  46.3 57.5 all-gather.1

commit v2 on v1

--- a/solution.py
+++ b/solution.py
@@ -13,13 +13,154 @@
 VMEM_LIMIT = 56 * 1024 * 1024
 
 
-def slot_places(targets, capacity):
+def slot_ranks(targets):
     order = jnp.arange(targets.shape[0])
     earlier = (targets[:, None] == targets[None, :]) & (order[None, :] < order[:, None])
-    return targets * capacity + jnp.sum(earlier.astype(jnp.int32), axis=1)
-
-
-def down_kernel(device_count, row_ref, column_ref, variant_ref, all_ref, own_ref, weight_ref, block_ref, out_ref, acc):
+    return jnp.sum(earlier.astype(jnp.int32), axis=1)
+
+
+def code_table(targets, ranks, codes, device_count, capacity):
+    places = jnp.arange(device_count * capacity)
+    hit = places[:, None] == (targets * capacity + ranks)[None, :]
+    return jnp.sum(jnp.where(hit, codes[None, :], 0), axis=1).reshape(device_count, capacity)
+
+
+VMEM = pl.BlockSpec(memory_space=pltpu.VMEM)
+SMEM = pl.BlockSpec(memory_space=pltpu.SMEM)
+
+
+def product_kernel(target_ref, slot_ref, row_ref, prompt_ref, block_ref, code_ref, out_ref):
+    count = out_ref.shape[1] - 16
+    out_ref[:, :count, :] = jnp.zeros((out_ref.shape[0], count, out_ref.shape[2]), jnp.bfloat16)
+    out_ref[:, count:, :] = code_ref[...]
+    batch = 8
+
+    def body(step, _):
+        parts = []
+        for i in range(batch):
+            j = step * batch + i
+            columns = pl.ds(pl.multiple_of(row_ref[j] * 128, 128), 128)
+            parts.append((j, jnp.dot(prompt_ref[:, columns], block_ref[j], preferred_element_type=jnp.float32)))
+        for j, part in parts:
+            rows = pl.ds(pl.multiple_of(slot_ref[j] * 16, 16), 16)
+            out_ref[target_ref[j], rows, :] = part.astype(jnp.bfloat16)
+        return 0
+
+    lax.fori_loop(0, block_ref.shape[0] // batch, body, 0)
+
+
+def exchange_kernel(device_count, with_base, *refs):
+    if with_base:
+        source, prompt_ref, gate_ref, up_ref, out_ref, gate_out, up_out, own_sem, send_sem, recv_sem = refs
+    else:
+        source, out_ref, own_sem, send_sem, recv_sem = refs
+    me = lax.axis_index("rows")
+
+    barrier = pltpu.get_barrier_semaphore()
+
+    def greet(k, _):
+        partner = lax.rem(me + k, device_count)
+        pl.semaphore_signal(barrier, inc=1, device_id={"rows": partner}, device_id_type=pl.DeviceIdType.MESH)
+        return 0
+
+    lax.fori_loop(1, device_count, greet, 0)
+    pl.semaphore_wait(barrier, device_count - 1)
+
+    def transfer(k, place):
+        partner = lax.rem(me + k, device_count)
+        return pltpu.make_async_remote_copy(
+            src_ref=source.at[partner],
+            dst_ref=out_ref.at[place],
+            send_sem=send_sem.at[k],
+            recv_sem=recv_sem.at[k],
+            device_id={"rows": partner},
+            device_id_type=pl.DeviceIdType.MESH,
+        )
+
+    def launch(k, _):
+        transfer(k, me).start()
+        return 0
+
+    lax.fori_loop(1, device_count, launch, 0)
+    own = pltpu.make_async_copy(source.at[me], out_ref.at[me], own_sem)
+    own.start()
+    if with_base:
+        tile = 1024
+        gate_out[...] = jnp.zeros_like(gate_out)
+        up_out[...] = jnp.zeros_like(up_out)
+
+        def base(step, _):
+            part = pl.ds(pl.multiple_of(step * tile, tile), tile)
+            chosen = prompt_ref[:, part]
+            gate_out[...] += jnp.dot(chosen, gate_ref[part, :], preferred_element_type=jnp.float32)
+            up_out[...] += jnp.dot(chosen, up_ref[part, :], preferred_element_type=jnp.float32)
+            return 0
+
+        lax.fori_loop(0, prompt_ref.shape[1] // tile, base, 0)
+    own.wait()
+
+    def finish(k, _):
+        copy = transfer(k, lax.rem(me - k + device_count, device_count))
+        copy.wait_recv()
+        copy.wait_send()
+        return 0
+
+    lax.fori_loop(1, device_count, finish, 0)
+
+
+def exchange(device_count, collective_id, source, base=()):
+    shapes = [jax.ShapeDtypeStruct(source.shape, source.dtype)]
+    if base:
+        tokens, width = base[0].shape[0], base[1].shape[1]
+        shapes += [jax.ShapeDtypeStruct((tokens, width), jnp.float32)] * 2
+    return pl.pallas_call(
+        functools.partial(exchange_kernel, device_count, bool(base)),
+        out_shape=shapes,
+        in_specs=[VMEM] * (1 + len(base)),
+        out_specs=[VMEM] * len(shapes),
+        scratch_shapes=[
+            pltpu.SemaphoreType.DMA,
+            pltpu.SemaphoreType.DMA((device_count,)),
+            pltpu.SemaphoreType.DMA((device_count,)),
+        ],
+        compiler_params=pltpu.CompilerParams(
+            collective_id=collective_id, has_side_effects=True, vmem_limit_bytes=VMEM_LIMIT
+        ),
+    )(source, *base)
+
+
+def hidden_kernel(capacity, code_ref, wish_ref, got_ref, gate_ref, up_ref, hidden_ref, reply_ref, sums):
+    sets = hidden_ref.shape[0] // 16
+    sums[...] = jnp.zeros_like(sums)
+
+    def add(device, _):
+        for slot in range(capacity):
+            code = code_ref[device, slot]
+            sums[code] += got_ref[device, slot * 16 : slot * 16 + 16, :].astype(jnp.float32)
+        return 0
+
+    lax.fori_loop(0, got_ref.shape[0], add, 0)
+
+    def finish(number, _):
+        live = (number > 0).astype(jnp.float32)
+        gate = gate_ref[...] + live * sums[2 * number]
+        up = up_ref[...] + live * sums[2 * number + 1]
+        rows = pl.ds(pl.multiple_of(number * 16, 16), 16)
+        hidden_ref[rows, :] = (jax.nn.silu(gate) * up).astype(jnp.bfloat16)
+        return 0
+
+    lax.fori_loop(0, sets, finish, 0)
+
+    def answer(device, _):
+        for slot in range(capacity):
+            rows = pl.ds(pl.multiple_of(wish_ref[device, slot] * 16, 16), 16)
+            reply_ref[device, slot * 16 : slot * 16 + 16, :] = hidden_ref[rows, :]
+        return 0
+
+    lax.fori_loop(0, reply_ref.shape[0], answer, 0)
+
+
+def down_kernel(device_count, row_ref, slot_ref, column_ref, variant_ref, all_ref, own_ref, weight_ref, block_ref, out_ref, acc):
     total_rows, model_width = acc.shape
     tile = 1024
 
@@ -37,7 +178,7 @@
         for i in range(batch):
             j = step * batch + i
             first = pl.multiple_of((variant_ref[j] + 1) * 16, 16)
-            rows = all_ref[row_ref[j], pl.ds(first, 16), :]
+            rows = all_ref[row_ref[j], pl.ds(pl.multiple_of(slot_ref[j] * 16, 16), 16), :]
             parts.append((j, first, jnp.dot(rows, block_ref[j], preferred_element_type=jnp.float32)))
         for j, first, part in parts:
             columns = pl.ds(pl.multiple_of(column_ref[j] * 128, 128), 128)
@@ -69,7 +210,7 @@
     lax.fori_loop(0, total_rows // 24, pack, 0)
 
 
-def down_partial(device_count, row, column, variant, gathered, own, weight, blocks):
+def down_partial(device_count, row, slot, column, variant, gathered, own, weight, blocks):
     total_rows = own.shape[0]
     model_width = weight.shape[1]
     width = model_width * (total_rows // device_count) // UNIT_ROWS
@@ -78,11 +219,11 @@
         out_shape=jax.ShapeDtypeStruct(
             (LANES, 2, device_count // 2, UNIT_ROWS, width // LANES), jnp.bfloat16
         ),
-        in_specs=[pl.BlockSpec(memory_space=pltpu.SMEM)] * 3 + [pl.BlockSpec(memory_space=pltpu.VMEM)] * 4,
+        in_specs=[pl.BlockSpec(memory_space=pltpu.SMEM)] * 4 + [pl.BlockSpec(memory_space=pltpu.VMEM)] * 4,
         out_specs=pl.BlockSpec(memory_space=pltpu.VMEM),
         scratch_shapes=[pltpu.VMEM((total_rows, model_width), jnp.float32)],
         compiler_params=pltpu.CompilerParams(vmem_limit_bytes=VMEM_LIMIT),
-    )(row, column, variant, gathered, own, weight, blocks)
+    )(row, slot, column, variant, gathered, own, weight, blocks)
 
 
 def bit_orders(device_count):
@@ -202,42 +343,45 @@
     device_count = lax.axis_size("rows")
     block_size = proj_blocks.shape[1]
     tokens, model_width = prompt.shape
-    width_blocks = model_width // block_size
     set_count = VARIANTS + 1
     slots = proj_blocks.shape[0]
     capacity = max(2, -(-slots // device_count))
-    places = device_count * capacity
-
-    prompt_blocks = prompt.reshape(tokens, width_blocks, block_size).transpose(1, 0, 2)
-    chosen = jnp.take(prompt_blocks, proj_row, axis=0)
-    products = jnp.einsum("spd,sdf->spf", chosen, proj_blocks, preferred_element_type=jnp.float32)
-    codes = (proj_variant * 2 + proj_kind + 2).astype(jnp.bfloat16)
-    payload = jnp.concatenate(
+
+    params = pltpu.CompilerParams(vmem_limit_bytes=VMEM_LIMIT)
+    proj_target, down_target = proj_column[:, 0], down_row[:, 0]
+    proj_slot, down_slot = slot_ranks(proj_target), slot_ranks(down_target)
+    codes = jnp.concatenate(
         [
-            products.astype(jnp.bfloat16).reshape(slots, tokens * block_size),
-            jnp.broadcast_to(codes[:, None], (slots, block_size)),
+            code_table(proj_target, proj_slot, proj_variant * 2 + proj_kind + 2, device_count, capacity),
+            code_table(down_target, down_slot, down_variant + 1, device_count, capacity),
+            jnp.zeros((device_count, block_size - 2 * capacity), jnp.int32),
         ],
         axis=1,
-    )
-    place_of = slot_places(proj_column[:, 0], capacity)
-    spread = (jnp.arange(places)[:, None] == place_of[None, :]).astype(jnp.bfloat16)
-    sent = jnp.dot(spread, payload, preferred_element_type=jnp.float32).astype(jnp.bfloat16)
-    got = lax.all_to_all(sent, "rows", split_axis=0, concat_axis=0, tiled=True)
-    got_codes = got[:, tokens * block_size].astype(jnp.int32)
-    values = got[:, : tokens * block_size]
-    pick = (got_codes[None, :] == jnp.arange(2 * set_count)[:, None]).astype(jnp.bfloat16)
-    pick = pick * (jnp.arange(2 * set_count)[:, None] >= 2).astype(jnp.bfloat16)
-    extra = jnp.dot(pick, values, preferred_element_type=jnp.float32)
-    extra = extra.reshape(set_count, 2, tokens, block_size)
-    gate_base = jnp.dot(prompt, gate_weight, preferred_element_type=jnp.float32)
-    up_base = jnp.dot(prompt, up_weight, preferred_element_type=jnp.float32)
-    gate_values = gate_base[None] + extra[:, 0]
-    up_values = up_base[None] + extra[:, 1]
-    hidden = (jax.nn.silu(gate_values) * up_values).astype(jnp.bfloat16)
-    hidden = hidden.reshape(set_count * tokens, block_size)
-    gathered = lax.all_gather(hidden, "rows", axis=0, tiled=False)
+    ).astype(jnp.bfloat16)
+    codes = jnp.broadcast_to(codes[:, None, :], (device_count, 16, block_size))
+    sent = pl.pallas_call(
+        product_kernel,
+        out_shape=jax.ShapeDtypeStruct((device_count, capacity * tokens + 16, block_size), jnp.bfloat16),
+        in_specs=[SMEM] * 3 + [VMEM] * 3,
+        out_specs=VMEM,
+        compiler_params=params,
+    )(proj_target, proj_slot, proj_row, prompt, proj_blocks, codes)
+    got, gate_base, up_base = exchange(device_count, 1, sent, (prompt, gate_weight, up_weight))
+    got_codes = got[:, capacity * tokens, : 2 * capacity].astype(jnp.int32)
+    hidden, reply = pl.pallas_call(
+        functools.partial(hidden_kernel, capacity),
+        out_shape=[
+            jax.ShapeDtypeStruct((set_count * tokens, block_size), jnp.bfloat16),
+            jax.ShapeDtypeStruct((device_count, capacity * tokens, block_size), jnp.bfloat16),
+        ],
+        in_specs=[SMEM] * 2 + [VMEM] * 3,
+        out_specs=[VMEM] * 2,
+        scratch_shapes=[pltpu.VMEM((2 * set_count, tokens, block_size), jnp.float32)],
+        compiler_params=params,
+    )(got_codes[:, :capacity], got_codes[:, capacity:], got, gate_base, up_base)
+    (gathered,) = exchange(device_count, 2, reply)
     part = down_partial(
-        device_count, down_row[:, 0], down_column, down_variant, gathered, hidden, down_weight, down_blocks
+        device_count, down_target, down_slot, down_column, down_variant, gathered, hidden, down_weight, down_blocks
     )
     chunk = reduce_scatter(device_count, part)
     own_rows = set_count * tokens // device_count

time: 173 us -> 117 us (0.68)
  waiting for transfers between devices: 70.4 us -> 0 us
  Pallas kernels: 59.4 us -> 108 us
  between operations: 13.6 us -> 0.13 us
  starting transfers between devices: 7.45 us -> 0 us
  matrix products: 6.78 us -> 0 us
  local copies, waits for them, and re-layouts: 8.93 us -> 5.05 us
  other arithmetic: 5.49 us -> 3.5 us
    all_gather x1 -> x0, waiting for transfers between devices: 57 us -> none  [on_device(): gathered = lax.all_gather(hidden, 'rows', axis=0, tiled=False)]
    pallas_call x0 -> x4, Pallas kernels: none -> 45.2 us  [the longest x2 36.9 us: exchange(): pl.pallas_call(functools.partial(exchange_kernel, device_count, bool(base...]
    all_to_all x1 -> x0, waiting for transfers between devices: 13.5 us -> none  [on_device(): got = lax.all_to_all(sent, 'rows', split_axis=0, concat_axis=0, tiled=True)]
    all_to_all x1 -> x0, starting transfers between devices: 7.41 us -> none  [on_device(): got = lax.all_to_all(sent, 'rows', split_axis=0, concat_axis=0, tiled=True)]
    dot_general x5 -> x0, matrix products: 6.78 us -> none  [the longest x1 2.12 us: on_device(): gate_base = jnp.dot(prompt, gate_weight, preferred_element_type=jnp.float32)]
    pallas_call x1, Pallas kernels: 47.3 us -> 51.8 us  [reduce_scatter(): pl.pallas_call(functools.partial(scatter_kernel, device_count), out_shape...]
    all_to_all x2 -> x0, local copies, waits for them, and re-layouts: 4.16 us -> none  [on_device(): got = lax.all_to_all(sent, 'rows', split_axis=0, concat_axis=0, tiled=True)]
    convert_element_type x5 -> x1, other arithmetic: 2.29 us -> 0.01 us  [on_device(): got_codes = got[:, capacity * tokens, :2 * capacity].astype(jnp.int32)]
  transfers between devices with their start and end apart: 2 -> 0, of which waited for: 2 -> 0; matrix products, arithmetic and copies ran while one was open for 2% -> 0% of each run, Pallas kernels for 0% -> 0%
where the time goes in v2:
time: 117 us
  Pallas kernels  108 us (92%)
  local copies, waits for them, and re-layouts  5.05 us (4%)
  other arithmetic  3.5 us (3%)
    pallas_call x1, Pallas kernels, reduce_scatter(): pl.pallas_call(functools.partial(scatter_kernel, device_count), out_shape...  51.8 us
    pallas_call x2, Pallas kernels, exchange(): pl.pallas_call(functools.partial(exchange_kernel, device_count, bool(base...  36.9 us
    pallas_call x1, Pallas kernels, down_partial(): pl.pallas_call(functools.partial(down_kernel, device_count), out_shape=ja...  11.3 us
    pallas_call x1, Pallas kernels, on_device(): pl.pallas_call(product_kernel, out_shape=jax.ShapeDtypeStruct((device_cou...  5.06 us
    pallas_call x1, Pallas kernels, on_device(): pl.pallas_call(functools.partial(hidden_kernel, capacity), out_shape=[jax...  3.22 us

profile of v2, /device:TPU:0, one launch (start us, length us, event | category | flops | bytes accessed | tf_op | source)
XLA Modules:
  0.0 116.9 jit_solution(1970818943216272621)
XLA Ops:
  0.0 0.9 convert_reduce_fusion.slot_ref
  0.9 0.0 copy-start.1
  0.9 0.9 convert_reduce_fusion.1.slot_ref
  1.8 0.0 copy-start
  1.9 0.1 pad.2.clone
  1.9 0.7 multiply_add_fusion
  2.6 0.1 select_reduce_fusion
  2.7 0.7 add_add_fusion
  3.4 0.1 select_reduce_fusion.1
  3.6 0.1 concatenate.12
  3.7 0.1 concatenate.13
  3.8 0.1 maximum_maximum_fusion
  3.9 0.7 broadcast_in_dim.41.code_ref
  4.6 0.0 copy-done.1
  4.6 5.1 %shard_map.127.refs_0_ = bf16[32,64,128]{2,1,0:T(8,128)(2,1)} custom-call(s32[96]{0:T(128)} %bitcast.16, s32[96]{0:T(128)} %copy-done.1, s32[96]{0:T(128)} %row_ref.1, bf16[16,8192]{1,0:T(8,128)(2,1)} %refs_1_.1, bf16[96,128,128]{2,1,0:T(8,128)(2,1)} %block_ref.2, bf16[32,16,128]{2,1,0:T(8,128)(2,1)} %broadcast_in_dim.41.code_ref), custom_call_target="tpu_custom_call" | custom-call | tf_op jit(solution)/shard_map/pallas_call | solution.py:362
  9.6 19.8 %shard_map.128 = (bf16[32,64,128]{2,1,0:T(8,128)(2,1)}, f32[16,128]{1,0:T(8,128)}, f32[16,128]{1,0:T(8,128)}) custom-call(bf16[32,64,128]{2,1,0:T(8,128)(2,1)} %shard_map.127.refs_0_, bf16[16,8192]{1,0:T(8,128)(2,1)} %refs_1_.1, bf16[8192,128]{1,0:T(8,128)(2,1)} %refs_2_.1, bf16[8192,128]{1,0:T(8,128)(2,1)} %refs_3_.1), custom_call_target="tpu_custom_call" | custom-call | tf_op jit(solution)/shard_map/pallas_call | solution.py:116
  29.4 0.0 copy-done
  29.5 1.4 %copy.21 = bf16[32,64,128]{2,0,1:T(8,128)(2,1)S(1)} copy(bf16[32,64,128]{2,1,0:T(8,128)(2,1)} %get-tuple-element.10.got_ref) | data formatting | bytes 1048576 | tf_op jit(solution)/shard_map/pallas_call | solution.py:116
  30.9 0.7 fusion.3
  31.5 3.2 %shard_map.129 = (bf16[384,128]{1,0:T(8,128)(2,1)}, bf16[32,48,128]{2,1,0:T(8,128)(2,1)}) custom-call(s32[32,3]{1,0:T(8,128)} %get-tuple-element.16.code_ref, s32[32,3]{1,0:T(8,128)} %get-tuple-element.15.wish_ref, bf16[32,64,128]{2,1,0:T(8,128)(2,1)} %get-tuple-element.10.got_ref, f32[16,128]{1,0:T(8,128)} %get-tuple-element.11.gate_ref, ...), custom_call_target="tpu_custom_call" | custom-call | tf_op jit(solution)/shard_map/pallas_call | solution.py:371
  34.7 17.1 %shard_map.130.all_ref = bf16[32,48,128]{2,1,0:T(8,128)(2,1)} custom-call(bf16[32,48,128]{2,1,0:T(8,128)(2,1)} %get-tuple-element.13.refs_0_), custom_call_target="tpu_custom_call" | custom-call | tf_op jit(solution)/shard_map/pallas_call | solution.py:116
  51.8 11.3 %shard_map.131.part_ref = bf16[4,2,16,48,512]{4,3,2,1,0:T(8,128)(2,1)} custom-call(s32[96]{0:T(128)} %bitcast.14, s32[96]{0:T(128)} %copy-done, s32[96]{0:T(128)} %column_ref.1, s32[96]{0:T(128)} %variant_ref.1, bf16[32,48,128]{2,1,0:T(8,128)(2,1)} %shard_map.130.all_ref, bf16[384,128]{1,0:T(8,128)(2,1)} %get-tuple-element.14.own_ref, ...), custom_call_target="tpu_custom_call" | custom-call | tf_op jit(solution)/shard_map/pallas_call | solution.py:217
  63.2 51.8 %shard_map.132 = bf16[4,48,512]{2,1,0:T(8,128)(2,1)} custom-call(bf16[4,2,16,48,512]{4,3,2,1,0:T(8,128)(2,1)} %shard_map.131.part_ref), custom_call_target="tpu_custom_call" | custom-call | tf_op jit(solution)/shard_map/pallas_call | solution.py:316
  114.9 1.1 copy.22
  116.0 0.1 copy.23
  116.1 0.8 reshape.54
  (4 shorter events, 0.0 us)
Async XLA Ops:
  0.9 3.7 %copy-start.1 = (s32[96]{0:T(128)}, s32[96]{0:T(128)S(1)}, u32[]{:S(2)}) copy-start(s32[96]{0:T(128)S(1)} %convert_reduce_fusion.slot_ref) | copy-start | bytes 1156
  1.8 27.6 %copy-start = (s32[96]{0:T(128)}, s32[96]{0:T(128)S(1)}, u32[]{:S(2)}) copy-start(s32[96]{0:T(128)S(1)} %convert_reduce_fusion.1.slot_ref) | copy-start | bytes 1156

commit v3 on v2

--- a/solution.py
+++ b/solution.py
@@ -9,7 +9,6 @@
 
 VARIANTS = 23
 UNIT_ROWS = 48
-LANES = 4
 VMEM_LIMIT = 56 * 1024 * 1024
 
 
@@ -189,14 +188,15 @@
     own_rows = total_rows // device_count
     pieces = UNIT_ROWS // own_rows
     width = model_width // pieces
-    narrow = width // LANES
+    lanes = lanes_of(width)
+    narrow = width // lanes
     owners = 24 // own_rows
 
     def pack(step, _):
         first = pl.multiple_of(step * 24, 24)
         for owner in range(owners):
             place = step * (owners // 2) + owner // 2
-            for channel in range(LANES):
+            for channel in range(lanes):
                 low = channel * narrow
                 parts = [
                     acc[pl.ds(first, 24), piece * width + low : piece * width + low + narrow][
@@ -217,7 +217,7 @@
     return pl.pallas_call(
         functools.partial(down_kernel, device_count),
         out_shape=jax.ShapeDtypeStruct(
-            (LANES, 2, device_count // 2, UNIT_ROWS, width // LANES), jnp.bfloat16
+            (lanes_of(width), 2, device_count // 2, UNIT_ROWS, width // lanes_of(width)), jnp.bfloat16
         ),
         in_specs=[pl.BlockSpec(memory_space=pltpu.SMEM)] * 4 + [pl.BlockSpec(memory_space=pltpu.VMEM)] * 4,
         out_specs=pl.BlockSpec(memory_space=pltpu.VMEM),
@@ -226,13 +226,18 @@
     )(row, slot, column, variant, gathered, own, weight, blocks)
 
 
+def lanes_of(width):
+    return min(8, width // 128)
+
+
 def bit_orders(device_count):
     if device_count == 32:
-        return [[0, 1, 2, 3, 4], [0, 2, 1, 3, 4]]
+        along_x, along_y = [0, 1, 2, 3, 4], [0, 2, 1, 3, 4]
+        return [[0, 3, 4, 1, 2], along_x, along_y, along_x, along_y, [0, 3, 4, 2, 1], along_x, along_y]
     bits = device_count.bit_length() - 1
     middle = (bits + 1) // 2
     first, second = list(range(1, middle)), list(range(middle, bits))
-    return [[0] + first + second, [0] + second + first]
+    return [[0] + first + second, [0] + second + first] * 4
 
 
 def scatter_kernel(device_count, part_ref, out_ref, *scratch):
@@ -243,7 +248,8 @@
     send_sem, recv_sem = scratch[3 * stages - 2 :]
     me = lax.axis_index("rows")
     half = device_count // 2
-    orders = [bit_orders(device_count)[c % 2] for c in range(LANES)]
+    lanes = part_ref.shape[0]
+    orders = bit_orders(device_count)[:lanes]
     my_bits = [(me // (1 << b)) % 2 for b in range(stages)]
     partners = [me + (1 - 2 * my_bits[b]) * (1 << b) for b in range(stages)]
 
@@ -264,12 +270,12 @@
         )
 
     copies = {}
-    for channel in range(LANES):
+    for channel in range(lanes):
         copies[channel, 0] = transfer(channel, 0)
         copies[channel, 0].start()
     for stage in range(stages):
         count = half >> stage
-        for channel in range(LANES):
+        for channel in range(lanes):
             copies[channel, stage].wait_recv()
 
             def value(i):
@@ -280,7 +286,11 @@
                 return mine + received[stage][channel, i].astype(jnp.float32)
 
             if stage == stages - 1:
-                out_ref[channel] = value(0).astype(jnp.bfloat16)
+                final = value(0)
+                own_rows, narrow = out_ref.shape[0], part_ref.shape[-1]
+                for piece in range(UNIT_ROWS // own_rows):
+                    low = (piece * lanes + channel) * narrow
+                    out_ref[:, low : low + narrow] = final[piece * own_rows : (piece + 1) * own_rows]
                 continue
             bit = orders[channel][stage + 1]
             low = 1 << sum(1 for other in orders[channel][stage + 2 :] if other < bit)
@@ -304,18 +314,18 @@
         copy.wait_send()
 
 
-def reduce_scatter(device_count, part):
-    narrow = part.shape[-1]
+def reduce_scatter(device_count, part, out_shape):
+    lanes, narrow = part.shape[0], part.shape[-1]
     stages = device_count.bit_length() - 1
     half = device_count // 2
     counts = [half >> s for s in range(stages)]
-    scratch = [pltpu.VMEM((LANES, k, UNIT_ROWS, narrow), jnp.bfloat16) for k in counts]
-    scratch += [pltpu.VMEM((LANES, k, UNIT_ROWS, narrow), jnp.bfloat16) for k in counts[1:]]
-    scratch += [pltpu.VMEM((LANES, k, UNIT_ROWS, narrow), jnp.float32) for k in counts[1:]]
-    scratch += [pltpu.SemaphoreType.DMA((LANES, stages))] * 2
+    scratch = [pltpu.VMEM((lanes, k, UNIT_ROWS, narrow), jnp.bfloat16) for k in counts]
+    scratch += [pltpu.VMEM((lanes, k, UNIT_ROWS, narrow), jnp.bfloat16) for k in counts[1:]]
+    scratch += [pltpu.VMEM((lanes, k, UNIT_ROWS, narrow), jnp.float32) for k in counts[1:]]
+    scratch += [pltpu.SemaphoreType.DMA((lanes, stages))] * 2
     return pl.pallas_call(
         functools.partial(scatter_kernel, device_count),
-        out_shape=jax.ShapeDtypeStruct((LANES, UNIT_ROWS, narrow), jnp.bfloat16),
+        out_shape=jax.ShapeDtypeStruct(out_shape, jnp.float32),
         in_specs=[pl.BlockSpec(memory_space=pltpu.VMEM)],
         out_specs=pl.BlockSpec(memory_space=pltpu.VMEM),
         scratch_shapes=scratch,
@@ -383,12 +393,8 @@
     part = down_partial(
         device_count, down_target, down_slot, down_column, down_variant, gathered, hidden, down_weight, down_blocks
     )
-    chunk = reduce_scatter(device_count, part)
     own_rows = set_count * tokens // device_count
-    pieces = UNIT_ROWS // own_rows
-    narrow = chunk.shape[-1]
-    chunk = chunk.reshape(LANES, pieces, own_rows, narrow).transpose(2, 1, 0, 3)
-    return chunk.reshape(own_rows, model_width)
+    return reduce_scatter(device_count, part, (own_rows, model_width)).astype(jnp.bfloat16)
 
 
 def solution(mesh):

time: 117 us -> 108 us (0.923)
  Pallas kernels: 108 us -> 99.2 us
  local copies, waits for them, and re-layouts: 5.05 us -> 3.06 us
  other arithmetic: 3.5 us -> 5.27 us
    pallas_call x1, Pallas kernels: 51.8 us -> 42.7 us  [reduce_scatter(): pl.pallas_call(functools.partial(scatter_kernel, device_count), out_shape...]
    convert_element_type x0 -> x1, other arithmetic: none -> 1.77 us  [on_device(): reduce_scatter(device_count, part, (own_rows, model_width))]
where the time goes in v3:
time: 108 us
  Pallas kernels  99.2 us (92%)
  other arithmetic  5.27 us (5%)
  local copies, waits for them, and re-layouts  3.06 us (3%)
    pallas_call x1, Pallas kernels, reduce_scatter(): pl.pallas_call(functools.partial(scatter_kernel, device_count), out_shape...  42.7 us
    pallas_call x2, Pallas kernels, exchange(): pl.pallas_call(functools.partial(exchange_kernel, device_count, bool(base...  36.9 us
    pallas_call x1, Pallas kernels, down_partial(): pl.pallas_call(functools.partial(down_kernel, device_count), out_shape=ja...  11.3 us
    pallas_call x1, Pallas kernels, on_device(): pl.pallas_call(product_kernel, out_shape=jax.ShapeDtypeStruct((device_cou...  5.06 us
    pallas_call x1, Pallas kernels, on_device(): pl.pallas_call(functools.partial(hidden_kernel, capacity), out_shape=[jax...  3.22 us

profile of v3, /device:TPU:0, one launch (start us, length us, event | category | flops | bytes accessed | tf_op | source)
XLA Modules:
  0.0 107.6 jit_solution(16738907204675523398)
XLA Ops:
  0.0 0.9 convert_reduce_fusion.slot_ref
  0.9 0.0 copy-start.1
  0.9 0.9 convert_reduce_fusion.1.slot_ref
  1.8 0.0 copy-start
  1.9 0.1 pad.2.clone
  1.9 0.7 multiply_add_fusion
  2.6 0.1 select_reduce_fusion
  2.7 0.7 add_add_fusion
  3.4 0.1 select_reduce_fusion.1
  3.6 0.1 concatenate.12
  3.7 0.1 concatenate.13
  3.8 0.1 maximum_maximum_fusion
  3.9 0.7 broadcast_in_dim.41.code_ref
  4.6 0.0 copy-done.1
  4.6 5.1 %shard_map.127.refs_0_ = bf16[32,64,128]{2,1,0:T(8,128)(2,1)} custom-call(s32[96]{0:T(128)} %bitcast.12, s32[96]{0:T(128)} %copy-done.1, s32[96]{0:T(128)} %row_ref.1, bf16[16,8192]{1,0:T(8,128)(2,1)} %refs_1_.1, bf16[96,128,128]{2,1,0:T(8,128)(2,1)} %block_ref.2, bf16[32,16,128]{2,1,0:T(8,128)(2,1)} %broadcast_in_dim.41.code_ref), custom_call_target="tpu_custom_call" | custom-call | tf_op jit(solution)/shard_map/pallas_call | solution.py:372
  9.6 19.8 %shard_map.128 = (bf16[32,64,128]{2,1,0:T(8,128)(2,1)}, f32[16,128]{1,0:T(8,128)}, f32[16,128]{1,0:T(8,128)}) custom-call(bf16[32,64,128]{2,1,0:T(8,128)(2,1)} %shard_map.127.refs_0_, bf16[16,8192]{1,0:T(8,128)(2,1)} %refs_1_.1, bf16[8192,128]{1,0:T(8,128)(2,1)} %refs_2_.1, bf16[8192,128]{1,0:T(8,128)(2,1)} %refs_3_.1), custom_call_target="tpu_custom_call" | custom-call | tf_op jit(solution)/shard_map/pallas_call | solution.py:115
  29.4 0.0 copy-done
  29.4 1.4 %copy.16 = bf16[32,64,128]{2,0,1:T(8,128)(2,1)S(1)} copy(bf16[32,64,128]{2,1,0:T(8,128)(2,1)} %get-tuple-element.10.got_ref) | data formatting | bytes 1048576 | tf_op jit(solution)/shard_map/pallas_call | solution.py:115
  30.8 0.7 fusion.3
  31.5 3.2 %shard_map.129 = (bf16[384,128]{1,0:T(8,128)(2,1)}, bf16[32,48,128]{2,1,0:T(8,128)(2,1)}) custom-call(s32[32,3]{1,0:T(8,128)} %get-tuple-element.16.code_ref, s32[32,3]{1,0:T(8,128)} %get-tuple-element.15.wish_ref, bf16[32,64,128]{2,1,0:T(8,128)(2,1)} %get-tuple-element.10.got_ref, f32[16,128]{1,0:T(8,128)} %get-tuple-element.11.gate_ref, ...), custom_call_target="tpu_custom_call" | custom-call | tf_op jit(solution)/shard_map/pallas_call | solution.py:381
  34.7 17.1 %shard_map.130.all_ref = bf16[32,48,128]{2,1,0:T(8,128)(2,1)} custom-call(bf16[32,48,128]{2,1,0:T(8,128)(2,1)} %get-tuple-element.13.refs_0_), custom_call_target="tpu_custom_call" | custom-call | tf_op jit(solution)/shard_map/pallas_call | solution.py:115
  51.8 11.3 %shard_map.131.part_ref = bf16[8,2,16,48,256]{4,3,2,1,0:T(8,128)(2,1)} custom-call(s32[96]{0:T(128)} %bitcast.10, s32[96]{0:T(128)} %copy-done, s32[96]{0:T(128)} %column_ref.1, s32[96]{0:T(128)} %variant_ref.1, bf16[32,48,128]{2,1,0:T(8,128)(2,1)} %shard_map.130.all_ref, bf16[384,128]{1,0:T(8,128)(2,1)} %get-tuple-element.14.own_ref, ...), custom_call_target="tpu_custom_call" | custom-call | tf_op jit(solution)/shard_map/pallas_call | solution.py:217
  63.1 42.7 %shard_map.132 = f32[12,8192]{1,0:T(8,128)} custom-call(bf16[8,2,16,48,256]{4,3,2,1,0:T(8,128)(2,1)} %shard_map.131.part_ref), custom_call_target="tpu_custom_call" | custom-call | tf_op jit(solution)/shard_map/pallas_call | solution.py:326
  105.9 1.8 %convert_element_type.24 = bf16[12,8192]{1,0:T(8,128)(2,1)} convert(f32[12,8192]{1,0:T(8,128)} %shard_map.132) | non-fusion elementwise | flops 98304 | bytes 589824 | tf_op jit(solution)/shard_map/convert_element_type | solution.py:397
  (4 shorter events, 0.0 us)
Async XLA Ops:
  0.9 3.7 %copy-start.1 = (s32[96]{0:T(128)}, s32[96]{0:T(128)S(1)}, u32[]{:S(2)}) copy-start(s32[96]{0:T(128)S(1)} %convert_reduce_fusion.slot_ref) | copy-start | bytes 1156
  1.8 27.6 %copy-start = (s32[96]{0:T(128)}, s32[96]{0:T(128)S(1)}, u32[]{:S(2)}) copy-start(s32[96]{0:T(128)S(1)} %convert_reduce_fusion.1.slot_ref) | copy-start | bytes 1156

commit v4 on v3

--- a/solution.py
+++ b/solution.py
@@ -9,7 +9,8 @@
 
 VARIANTS = 23
 UNIT_ROWS = 48
-VMEM_LIMIT = 56 * 1024 * 1024
+VMEM_LIMIT = 30 * 1024 * 1024
+SMALL_LIMIT = 10 * 1024 * 1024
 
 
 def slot_ranks(targets):
@@ -123,7 +124,7 @@
             pltpu.SemaphoreType.DMA((device_count,)),
         ],
         compiler_params=pltpu.CompilerParams(
-            collective_id=collective_id, has_side_effects=True, vmem_limit_bytes=VMEM_LIMIT
+            collective_id=collective_id, has_side_effects=True, vmem_limit_bytes=SMALL_LIMIT
         ),
     )(source, *base)
 
@@ -357,7 +358,7 @@
     slots = proj_blocks.shape[0]
     capacity = max(2, -(-slots // device_count))
 
-    params = pltpu.CompilerParams(vmem_limit_bytes=VMEM_LIMIT)
+    params = pltpu.CompilerParams(vmem_limit_bytes=SMALL_LIMIT)
     proj_target, down_target = proj_column[:, 0], down_row[:, 0]
     proj_slot, down_slot = slot_ranks(proj_target), slot_ranks(down_target)
     codes = jnp.concatenate(

time: 108 us -> 94 us (0.87)
  Pallas kernels: 99.2 us -> 82.7 us
  local copies, waits for them, and re-layouts: 3.06 us -> 6.52 us
    unnamed x4 -> x24, local copies, waits for them, and re-layouts: 0.01 us -> 5.76 us
    pallas_call x2, Pallas kernels: 36.9 us -> 32 us  [exchange(): pl.pallas_call(functools.partial(exchange_kernel, device_count, bool(base...]
    pallas_call x1, Pallas kernels: 11.3 us -> 6.52 us  [down_partial(): pl.pallas_call(functools.partial(down_kernel, device_count), out_shape=ja...]
    pallas_call x1, Pallas kernels: 42.7 us -> 39.2 us  [reduce_scatter(): pl.pallas_call(functools.partial(scatter_kernel, device_count), out_shape...]
    pallas_call x1, Pallas kernels: 5.06 us -> 2.85 us  [on_device(): pl.pallas_call(product_kernel, out_shape=jax.ShapeDtypeStruct((device_cou...]
where the time goes in v4:
time: 94 us; the launch traced here: 93.7 us
  Pallas kernels  82.7 us (88%)
  local copies, waits for them, and re-layouts  6.52 us (7%)
  other arithmetic  4.24 us (5%)
    pallas_call x1, Pallas kernels, reduce_scatter(): pl.pallas_call(functools.partial(scatter_kernel, device_count), out_shape...  39.2 us
    pallas_call x2, Pallas kernels, exchange(): pl.pallas_call(functools.partial(exchange_kernel, device_count, bool(base...  32 us
    pallas_call x1, Pallas kernels, down_partial(): pl.pallas_call(functools.partial(down_kernel, device_count), out_shape=ja...  6.52 us
    unnamed x24, local copies, waits for them, and re-layouts  5.76 us
    pallas_call x1, Pallas kernels, on_device(): pl.pallas_call(product_kernel, out_shape=jax.ShapeDtypeStruct((device_cou...  2.85 us
    pallas_call x1, Pallas kernels, on_device(): pl.pallas_call(functools.partial(hidden_kernel, capacity), out_shape=[jax...  2.15 us

profile of v4, /device:TPU:0, one launch (start us, length us, event | category | flops | bytes accessed | tf_op | source)
XLA Modules:
  0.0 93.7 jit_solution(5382484191827065214)
XLA Ops:
  0.0 0.9 convert_reduce_fusion.slot_ref
  0.9 0.9 convert_reduce_fusion.1.slot_ref
  1.8 0.1 pad.2.clone
  1.9 0.7 multiply_add_fusion
  2.6 0.1 select_reduce_fusion
  2.7 0.7 add_add_fusion
  3.4 0.1 select_reduce_fusion.1
  3.5 0.1 concatenate.12
  3.7 0.1 concatenate.13
  3.8 0.1 maximum_maximum_fusion
  3.9 0.0 copy-start
  3.9 1.9 %copy-done = bf16[96,128,128]{2,1,0:T(8,128)(2,1)S(1)} copy-done((bf16[96,128,128]{2,1,0:T(8,128)(2,1)S(1)}, bf16[96,128,128]{2,1,0:T(8,128)(2,1)}, u32[]{:S(2)}) %copy-start) | copy-done | bytes 3145752
  5.8 0.9 %copy-done.5 = bf16[16,8192]{1,0:T(8,128)(2,1)S(1)} copy-done((bf16[16,8192]{1,0:T(8,128)(2,1)S(1)}, bf16[16,8192]{1,0:T(8,128)(2,1)}, u32[]{:S(2)}) %copy-start.5) | copy-done | bytes 262168
  6.7 0.7 copy-done.9
  7.4 0.7 copy-done.10
  8.1 2.8 %shard_map.127.refs_0_ = bf16[32,64,128]{2,1,0:T(8,128)(2,1)S(1)} custom-call(s32[96]{0:T(128)S(1)} %bitcast.12, s32[96]{0:T(128)S(1)} %convert_reduce_fusion.slot_ref, s32[96]{0:T(128)S(1)} %copy-done.10, bf16[16,8192]{1,0:T(8,128)(2,1)S(1)} %copy-done.5, bf16[96,128,128]{2,1,0:T(8,128)(2,1)S(1)} %copy-done, bf16[32,16,128]{2,1,0:T(8,128)(2,1)S(1)} %broadcast_in_dim.41.code_ref), custom_call_target="tpu_custom_call" | custom-call | tf_op jit(solution)/shard_map/pallas_call | solution.py:373
  10.9 0.0 copy-done.3
  10.9 0.0 copy-done.6
  10.9 0.0 copy-start.4
  10.9 1.6 %copy-done.4 = bf16[8192,128]{1,0:T(8,128)(2,1)S(1)} copy-done((bf16[8192,128]{1,0:T(8,128)(2,1)S(1)}, bf16[8192,128]{1,0:T(8,128)(2,1)}, u32[]{:S(2)}) %copy-start.4) | copy-done | bytes 2097176
  12.5 0.0 copy-start.11
  12.6 16.6 %shard_map.128 = (bf16[32,64,128]{2,1,0:T(8,128)(2,1)S(1)}, f32[16,128]{1,0:T(8,128)S(1)}, f32[16,128]{1,0:T(8,128)S(1)}) custom-call(bf16[32,64,128]{2,1,0:T(8,128)(2,1)S(1)} %shard_map.127.refs_0_, bf16[16,8192]{1,0:T(8,128)(2,1)S(1)} %copy-done.6, bf16[8192,128]{1,0:T(8,128)(2,1)S(1)} %copy-done.3, bf16[8192,128]{1,0:T(8,128)(2,1)S(1)} %copy-done.4), custom_call_target="tpu_custom_call" | custom-call | tf_op jit(solution)/shard_map/pallas_call | solution.py:116
  29.1 0.3 copy.16
  29.5 0.1 fusion.3
  29.6 2.1 %shard_map.129 = (bf16[384,128]{1,0:T(8,128)(2,1)S(1)}, bf16[32,48,128]{2,1,0:T(8,128)(2,1)S(1)}) custom-call(s32[32,3]{1,0:T(8,128)S(1)} %get-tuple-element.16.code_ref, s32[32,3]{1,0:T(8,128)S(1)} %get-tuple-element.15.wish_ref, bf16[32,64,128]{2,1,0:T(8,128)(2,1)S(1)} %get-tuple-element.10.got_ref, f32[16,128]{1,0:T(8,128)S(1)} %get-tuple-element.11.gate_ref, ...), custom_call_target="tpu_custom_call" | custom-call | tf_op jit(solution)/shard_map/pallas_call | solution.py:382
  31.7 15.4 %shard_map.130.all_ref = bf16[32,48,128]{2,1,0:T(8,128)(2,1)S(1)} custom-call(bf16[32,48,128]{2,1,0:T(8,128)(2,1)S(1)} %get-tuple-element.13.refs_0_), custom_call_target="tpu_custom_call" | custom-call | tf_op jit(solution)/shard_map/pallas_call | solution.py:116
  47.1 0.0 copy-done.1
  47.1 0.0 copy-done.2
  47.1 0.0 copy-done.7
  47.2 6.5 %shard_map.131.part_ref = bf16[8,2,16,48,256]{4,3,2,1,0:T(8,128)(2,1)S(1)} custom-call(s32[96]{0:T(128)S(1)} %bitcast.10, s32[96]{0:T(128)S(1)} %convert_reduce_fusion.1.slot_ref, s32[96]{0:T(128)S(1)} %copy-done.11, s32[96]{0:T(128)S(1)} %copy-done.8, bf16[32,48,128]{2,1,0:T(8,128)(2,1)S(1)} %shard_map.130.all_ref, ...), custom_call_target="tpu_custom_call" | custom-call | tf_op jit(solution)/shard_map/pallas_call | solution.py:218
  53.7 39.2 %shard_map.132 = f32[12,8192]{1,0:T(8,128)S(1)} custom-call(bf16[8,2,16,48,256]{4,3,2,1,0:T(8,128)(2,1)S(1)} %shard_map.131.part_ref), custom_call_target="tpu_custom_call" | custom-call | tf_op jit(solution)/shard_map/pallas_call | solution.py:327
  93.0 0.7 convert_element_type.24
  (16 shorter events, 0.1 us)
Async XLA Ops:
  3.9 1.9 %copy-start = (bf16[96,128,128]{2,1,0:T(8,128)(2,1)S(1)}, bf16[96,128,128]{2,1,0:T(8,128)(2,1)}, u32[]{:S(2)}) copy-start(bf16[96,128,128]{2,1,0:T(8,128)(2,1)} %block_ref.2) | copy-start | bytes 9437188
  5.8 0.9 %copy-start.5 = (bf16[16,8192]{1,0:T(8,128)(2,1)S(1)}, bf16[16,8192]{1,0:T(8,128)(2,1)}, u32[]{:S(2)}) copy-start(bf16[16,8192]{1,0:T(8,128)(2,1)} %refs_1_.1) | copy-start | bytes 786436
  6.7 0.7 copy-start.9
  7.4 0.7 copy-start.10
  8.1 2.9 %copy-start.3 = (bf16[8192,128]{1,0:T(8,128)(2,1)S(1)}, bf16[8192,128]{1,0:T(8,128)(2,1)}, u32[]{:S(2)}) copy-start(bf16[8192,128]{1,0:T(8,128)(2,1)} %refs_2_.1) | copy-start | bytes 6291460
  8.1 2.9 %copy-start.6 = (bf16[16,8192]{1,0:T(8,128)(2,1)S(1)}, bf16[16,8192]{1,0:T(8,128)(2,1)}, u32[]{:S(2)}) copy-start(bf16[16,8192]{1,0:T(8,128)(2,1)} %refs_1_.1) | copy-start | bytes 786436
  10.9 1.6 %copy-start.4 = (bf16[8192,128]{1,0:T(8,128)(2,1)S(1)}, bf16[8192,128]{1,0:T(8,128)(2,1)}, u32[]{:S(2)}) copy-start(bf16[8192,128]{1,0:T(8,128)(2,1)} %refs_3_.1) | copy-start | bytes 6291460
  12.5 34.6 %copy-start.1 = (bf16[96,128,128]{2,1,0:T(8,128)(2,1)S(1)}, bf16[96,128,128]{2,1,0:T(8,128)(2,1)}, u32[]{:S(2)}) copy-start(bf16[96,128,128]{2,1,0:T(8,128)(2,1)} %block_ref.3) | copy-start | bytes 9437188
  12.5 34.6 %copy-start.2 = (bf16[128,8192]{1,0:T(8,128)(2,1)S(1)}, bf16[128,8192]{1,0:T(8,128)(2,1)}, u32[]{:S(2)}) copy-start(bf16[128,8192]{1,0:T(8,128)(2,1)} %weight_ref.1) | copy-start | bytes 6291460
  12.5 34.6 %copy-start.7 = (s32[96,1]{0,1:T(1,128)S(1)}, s32[96,1]{0,1:T(1,128)}, u32[]{:S(2)}) copy-start(s32[96,1]{0,1:T(1,128)} %param.23) | copy-start | bytes 1156
  12.5 34.6 %copy-start.8 = (s32[96]{0:T(128)S(1)}, s32[96]{0:T(128)}, u32[]{:S(2)}) copy-start(s32[96]{0:T(128)} %variant_ref.1) | copy-start | bytes 1156
  12.5 34.6 %copy-start.11 = (s32[96]{0:T(128)S(1)}, s32[96]{0:T(128)}, u32[]{:S(2)}) copy-start(s32[96]{0:T(128)} %column_ref.1) | copy-start | bytes 1156

commit v5 on v4

--- a/solution.py
+++ b/solution.py
@@ -274,43 +274,44 @@
     for channel in range(lanes):
         copies[channel, 0] = transfer(channel, 0)
         copies[channel, 0].start()
-    for stage in range(stages):
+    steps = [(stage, channel) for stage in range(stages) for channel in range(lanes)]
+    steps.sort(key=lambda step: (step[0] > 0, 4 * step[0] + step[1], step[0]))
+    for stage, channel in steps:
         count = half >> stage
-        for channel in range(lanes):
-            copies[channel, stage].wait_recv()
-
-            def value(i):
-                if stage == 0:
-                    mine = part_ref[channel, my_bits[0], i].astype(jnp.float32)
-                else:
-                    mine = kept[stage][channel, i]
-                return mine + received[stage][channel, i].astype(jnp.float32)
-
-            if stage == stages - 1:
-                final = value(0)
-                own_rows, narrow = out_ref.shape[0], part_ref.shape[-1]
-                for piece in range(UNIT_ROWS // own_rows):
-                    low = (piece * lanes + channel) * narrow
-                    out_ref[:, low : low + narrow] = final[piece * own_rows : (piece + 1) * own_rows]
-                continue
-            bit = orders[channel][stage + 1]
-            low = 1 << sum(1 for other in orders[channel][stage + 2 :] if other < bit)
-
-            def pick(j, side):
-                return (j // low) * (2 * low) + side * low + j % low
-
-            def send_side(j, _):
-                sending[stage + 1][channel, j] = value(pick(j, 1 - my_bits[bit])).astype(jnp.bfloat16)
-                return 0
-
-            def keep_side(j, _):
-                kept[stage + 1][channel, j] = value(pick(j, my_bits[bit]))
-                return 0
-
-            lax.fori_loop(0, count // 2, send_side, 0)
-            copies[channel, stage + 1] = transfer(channel, stage + 1)
-            copies[channel, stage + 1].start()
-            lax.fori_loop(0, count // 2, keep_side, 0)
+        copies[channel, stage].wait_recv()
+
+        def value(i):
+            if stage == 0:
+                mine = part_ref[channel, my_bits[0], i].astype(jnp.float32)
+            else:
+                mine = kept[stage][channel, i]
+            return mine + received[stage][channel, i].astype(jnp.float32)
+
+        if stage == stages - 1:
+            final = value(0)
+            own_rows, narrow = out_ref.shape[0], part_ref.shape[-1]
+            for piece in range(UNIT_ROWS // own_rows):
+                low = (piece * lanes + channel) * narrow
+                out_ref[:, low : low + narrow] = final[piece * own_rows : (piece + 1) * own_rows]
+            continue
+        bit = orders[channel][stage + 1]
+        low = 1 << sum(1 for other in orders[channel][stage + 2 :] if other < bit)
+
+        def pick(j, side):
+            return (j // low) * (2 * low) + side * low + j % low
+
+        def send_side(j, _):
+            sending[stage + 1][channel, j] = value(pick(j, 1 - my_bits[bit])).astype(jnp.bfloat16)
+            return 0
+
+        def keep_side(j, _):
+            kept[stage + 1][channel, j] = value(pick(j, my_bits[bit]))
+            return 0
+
+        lax.fori_loop(0, count // 2, send_side, 0)
+        copies[channel, stage + 1] = transfer(channel, stage + 1)
+        copies[channel, stage + 1].start()
+        lax.fori_loop(0, count // 2, keep_side, 0)
     for copy in copies.values():
         copy.wait_send()
 

time: 94 us -> 93.7 us (level)
  no operation moved by 1% of the time
where the time goes in v5:
time: 93.7 us; the launch traced here: 93.5 us
  Pallas kernels  82.5 us (88%)
  local copies, waits for them, and re-layouts  6.52 us (7%)
  other arithmetic  4.24 us (5%)
    pallas_call x1, Pallas kernels, reduce_scatter(): pl.pallas_call(functools.partial(scatter_kernel, device_count), out_shape...  39 us
    pallas_call x2, Pallas kernels, exchange(): pl.pallas_call(functools.partial(exchange_kernel, device_count, bool(base...  32 us
    pallas_call x1, Pallas kernels, down_partial(): pl.pallas_call(functools.partial(down_kernel, device_count), out_shape=ja...  6.53 us
    unnamed x24, local copies, waits for them, and re-layouts  5.76 us
    pallas_call x1, Pallas kernels, on_device(): pl.pallas_call(product_kernel, out_shape=jax.ShapeDtypeStruct((device_cou...  2.85 us
    pallas_call x1, Pallas kernels, on_device(): pl.pallas_call(functools.partial(hidden_kernel, capacity), out_shape=[jax...  2.15 us

profile of v5, /device:TPU:0, one launch (start us, length us, event | category | flops | bytes accessed | tf_op | source)
XLA Modules:
  0.0 93.5 jit_solution(10168525395398784156)
XLA Ops:
  0.0 0.9 convert_reduce_fusion.slot_ref
  0.9 0.9 convert_reduce_fusion.1.slot_ref
  1.8 0.1 pad.2.clone
  1.9 0.7 multiply_add_fusion
  2.6 0.1 select_reduce_fusion
  2.7 0.7 add_add_fusion
  3.4 0.1 select_reduce_fusion.1
  3.5 0.1 concatenate.12
  3.7 0.1 concatenate.13
  3.8 0.1 maximum_maximum_fusion
  3.9 0.0 copy-start
  3.9 1.9 %copy-done = bf16[96,128,128]{2,1,0:T(8,128)(2,1)S(1)} copy-done((bf16[96,128,128]{2,1,0:T(8,128)(2,1)S(1)}, bf16[96,128,128]{2,1,0:T(8,128)(2,1)}, u32[]{:S(2)}) %copy-start) | copy-done | bytes 3145752
  5.8 0.9 %copy-done.5 = bf16[16,8192]{1,0:T(8,128)(2,1)S(1)} copy-done((bf16[16,8192]{1,0:T(8,128)(2,1)S(1)}, bf16[16,8192]{1,0:T(8,128)(2,1)}, u32[]{:S(2)}) %copy-start.5) | copy-done | bytes 262168
  6.7 0.7 copy-done.9
  7.4 0.7 copy-done.10
  8.1 2.8 %shard_map.127.refs_0_ = bf16[32,64,128]{2,1,0:T(8,128)(2,1)S(1)} custom-call(s32[96]{0:T(128)S(1)} %bitcast.12, s32[96]{0:T(128)S(1)} %convert_reduce_fusion.slot_ref, s32[96]{0:T(128)S(1)} %copy-done.10, bf16[16,8192]{1,0:T(8,128)(2,1)S(1)} %copy-done.5, bf16[96,128,128]{2,1,0:T(8,128)(2,1)S(1)} %copy-done, bf16[32,16,128]{2,1,0:T(8,128)(2,1)S(1)} %broadcast_in_dim.41.code_ref), custom_call_target="tpu_custom_call" | custom-call | tf_op jit(solution)/shard_map/pallas_call | solution.py:374
  10.9 0.0 copy-done.3
  10.9 0.0 copy-done.6
  10.9 0.0 copy-start.4
  10.9 1.6 %copy-done.4 = bf16[8192,128]{1,0:T(8,128)(2,1)S(1)} copy-done((bf16[8192,128]{1,0:T(8,128)(2,1)S(1)}, bf16[8192,128]{1,0:T(8,128)(2,1)}, u32[]{:S(2)}) %copy-start.4) | copy-done | bytes 2097176
  12.5 0.0 copy-start.11
  12.6 16.5 %shard_map.128 = (bf16[32,64,128]{2,1,0:T(8,128)(2,1)S(1)}, f32[16,128]{1,0:T(8,128)S(1)}, f32[16,128]{1,0:T(8,128)S(1)}) custom-call(bf16[32,64,128]{2,1,0:T(8,128)(2,1)S(1)} %shard_map.127.refs_0_, bf16[16,8192]{1,0:T(8,128)(2,1)S(1)} %copy-done.6, bf16[8192,128]{1,0:T(8,128)(2,1)S(1)} %copy-done.3, bf16[8192,128]{1,0:T(8,128)(2,1)S(1)} %copy-done.4), custom_call_target="tpu_custom_call" | custom-call | tf_op jit(solution)/shard_map/pallas_call | solution.py:116
  29.1 0.3 copy.16
  29.5 0.1 fusion.3
  29.5 2.1 %shard_map.129 = (bf16[384,128]{1,0:T(8,128)(2,1)S(1)}, bf16[32,48,128]{2,1,0:T(8,128)(2,1)S(1)}) custom-call(s32[32,3]{1,0:T(8,128)S(1)} %get-tuple-element.16.code_ref, s32[32,3]{1,0:T(8,128)S(1)} %get-tuple-element.15.wish_ref, bf16[32,64,128]{2,1,0:T(8,128)(2,1)S(1)} %get-tuple-element.10.got_ref, f32[16,128]{1,0:T(8,128)S(1)} %get-tuple-element.11.gate_ref, ...), custom_call_target="tpu_custom_call" | custom-call | tf_op jit(solution)/shard_map/pallas_call | solution.py:383
  31.7 15.4 %shard_map.130.all_ref = bf16[32,48,128]{2,1,0:T(8,128)(2,1)S(1)} custom-call(bf16[32,48,128]{2,1,0:T(8,128)(2,1)S(1)} %get-tuple-element.13.refs_0_), custom_call_target="tpu_custom_call" | custom-call | tf_op jit(solution)/shard_map/pallas_call | solution.py:116
  47.1 0.0 copy-done.1
  47.1 0.0 copy-done.2
  47.1 0.0 copy-done.7
  47.2 6.5 %shard_map.131.part_ref = bf16[8,2,16,48,256]{4,3,2,1,0:T(8,128)(2,1)S(1)} custom-call(s32[96]{0:T(128)S(1)} %bitcast.10, s32[96]{0:T(128)S(1)} %convert_reduce_fusion.1.slot_ref, s32[96]{0:T(128)S(1)} %copy-done.11, s32[96]{0:T(128)S(1)} %copy-done.8, bf16[32,48,128]{2,1,0:T(8,128)(2,1)S(1)} %shard_map.130.all_ref, ...), custom_call_target="tpu_custom_call" | custom-call | tf_op jit(solution)/shard_map/pallas_call | solution.py:218
  53.7 39.0 %shard_map.132 = f32[12,8192]{1,0:T(8,128)S(1)} custom-call(bf16[8,2,16,48,256]{4,3,2,1,0:T(8,128)(2,1)S(1)} %shard_map.131.part_ref), custom_call_target="tpu_custom_call" | custom-call | tf_op jit(solution)/shard_map/pallas_call | solution.py:328
  92.7 0.7 convert_element_type.24
  (16 shorter events, 0.1 us)
Async XLA Ops:
  3.9 1.9 %copy-start = (bf16[96,128,128]{2,1,0:T(8,128)(2,1)S(1)}, bf16[96,128,128]{2,1,0:T(8,128)(2,1)}, u32[]{:S(2)}) copy-start(bf16[96,128,128]{2,1,0:T(8,128)(2,1)} %block_ref.2) | copy-start | bytes 9437188
  5.8 0.9 %copy-start.5 = (bf16[16,8192]{1,0:T(8,128)(2,1)S(1)}, bf16[16,8192]{1,0:T(8,128)(2,1)}, u32[]{:S(2)}) copy-start(bf16[16,8192]{1,0:T(8,128)(2,1)} %refs_1_.1) | copy-start | bytes 786436
  6.7 0.7 copy-start.9
  7.4 0.7 copy-start.10
  8.1 2.9 %copy-start.3 = (bf16[8192,128]{1,0:T(8,128)(2,1)S(1)}, bf16[8192,128]{1,0:T(8,128)(2,1)}, u32[]{:S(2)}) copy-start(bf16[8192,128]{1,0:T(8,128)(2,1)} %refs_2_.1) | copy-start | bytes 6291460
  8.1 2.9 %copy-start.6 = (bf16[16,8192]{1,0:T(8,128)(2,1)S(1)}, bf16[16,8192]{1,0:T(8,128)(2,1)}, u32[]{:S(2)}) copy-start(bf16[16,8192]{1,0:T(8,128)(2,1)} %refs_1_.1) | copy-start | bytes 786436
  10.9 1.6 %copy-start.4 = (bf16[8192,128]{1,0:T(8,128)(2,1)S(1)}, bf16[8192,128]{1,0:T(8,128)(2,1)}, u32[]{:S(2)}) copy-start(bf16[8192,128]{1,0:T(8,128)(2,1)} %refs_3_.1) | copy-start | bytes 6291460
  12.5 34.6 %copy-start.1 = (bf16[96,128,128]{2,1,0:T(8,128)(2,1)S(1)}, bf16[96,128,128]{2,1,0:T(8,128)(2,1)}, u32[]{:S(2)}) copy-start(bf16[96,128,128]{2,1,0:T(8,128)(2,1)} %block_ref.3) | copy-start | bytes 9437188
  12.5 34.6 %copy-start.2 = (bf16[128,8192]{1,0:T(8,128)(2,1)S(1)}, bf16[128,8192]{1,0:T(8,128)(2,1)}, u32[]{:S(2)}) copy-start(bf16[128,8192]{1,0:T(8,128)(2,1)} %weight_ref.1) | copy-start | bytes 6291460
  12.5 34.6 %copy-start.7 = (s32[96,1]{0,1:T(1,128)S(1)}, s32[96,1]{0,1:T(1,128)}, u32[]{:S(2)}) copy-start(s32[96,1]{0,1:T(1,128)} %param.23) | copy-start | bytes 1156
  12.5 34.6 %copy-start.8 = (s32[96]{0:T(128)S(1)}, s32[96]{0:T(128)}, u32[]{:S(2)}) copy-start(s32[96]{0:T(128)} %variant_ref.1) | copy-start | bytes 1156
  12.5 34.6 %copy-start.11 = (s32[96]{0:T(128)S(1)}, s32[96]{0:T(128)}, u32[]{:S(2)}) copy-start(s32[96]{0:T(128)} %column_ref.1) | copy-start | bytes 1156
